TPU v7x, 256 devices: a whole 4x4x8 slice. The times are simulated.
256 devices in a mesh: dp: 8 (over y, core), fsdp: 32 (over x, z).
Axes of the slice: x: 4, y: 4, z: 8, core: 2. Of those that a mesh axis runs over, the one named last changes fastest.
Arguments:
- kva_parts: bfloat16 [8, 576, 7168], P('dp', 'fsdp'), may hold values from -60 to 60
- kvb_parts: bfloat16 [8, 16384, 512], P('dp', 'fsdp'), may hold values from -60 to 60
- kva_moment: float32 [576, 7168], P('fsdp'), may hold values from -60 to 60
- kvb_moment: float32 [16384, 512], P('fsdp'), may hold values from -60 to 60
Outputs:
- kva_moment_new: float32 [576, 7168], P('fsdp')
- kvb_moment_new: float32 [16384, 512], P('fsdp')
- kva_update: bfloat16 [576, 7168], P('fsdp')
- kvb_update: bfloat16 [16384, 512], P('fsdp')
All inputs are finite; a program needn't handle non-finite values.
Results may differ from a plain program's by a relative error of at most 0.035.
Values may be sent and summed in bfloat16 or wider, within the bound.
No kernel may reach another device: no remote copies, remote signals or barrier semaphores. Data moves between devices by JAX's collectives and lax.ppermute only.
A program may use at most 64 MiB of HBM per device.

v0:
```python
import functools
import math

import jax
import jax.numpy as jnp
from jax import lax
from jax.experimental import pallas as pl
from jax.experimental.pallas import tpu as pltpu
from jax.sharding import Mesh, PartitionSpec as P

D = 7168
KV_RANK = 512
KVA_ROWS = 576
KVB_ROWS = 16384
DP = ("y", "c")
FSDP = ("x", "z")
N_DP = 8
N_FSDP = 32
CHUNK = D // N_DP
GROUPS = CHUNK // 128
MAIN = 16
WIDE = CHUNK + 128
BLOCKS = 5

c1 = 3.4445
c2 = -4.775
c3 = 2.0315
decay_rate = 0.95
norm_epsilon = 1e-07
f32 = jnp.float32
bf16 = jnp.bfloat16
VMEM_LIMIT = 48 * 1024 * 1024
HINT = 40_000_000_000


def call(body, out_shape, n_scalar=0, n_in=1, scratch=(), space=pltpu.VMEM, limit=VMEM_LIMIT, flops=0):
    return pl.pallas_call(
        body,
        out_shape=out_shape,
        in_specs=[pl.BlockSpec(memory_space=pltpu.SMEM)] * n_scalar
        + [pl.BlockSpec(memory_space=space)] * n_in,
        out_specs=jax.tree.map(lambda _: pl.BlockSpec(memory_space=pltpu.VMEM), out_shape),
        scratch_shapes=list(scratch),
        compiler_params=pltpu.CompilerParams(vmem_limit_bytes=limit),
        cost_estimate=pl.CostEstimate(flops=flops, bytes_accessed=0, transcendentals=0)
        if flops
        else None,
    )


def shape(dims, dtype):
    return jax.ShapeDtypeStruct(dims, dtype)


def tail_tile(rows):
    pieces = [rows[:, 128 * k : 128 * k + 128] for k in range(GROUPS)]
    return jnp.concatenate(pieces + [jnp.zeros((2, 128), f32)], axis=0)


def pack_body(c_ref, a_ref, b_ref, o_ref, send_ref, held_ref, sems):
    rows = send_ref.shape[0]
    other = pl.ds(pl.multiple_of((1 - c_ref[0]) * rows, rows), rows)
    copy_a = pltpu.make_async_copy(a_ref, held_ref, sems.at[0])
    copy_b = pltpu.make_async_copy(b_ref.at[0, other], send_ref, sems.at[1])
    copy_a.start()
    copy_b.start()
    copy_a.wait()
    for d in range(N_DP):
        lanes = slice(d * CHUNK, (d + 1) * CHUNK)
        o_ref[d, :, :CHUNK] = held_ref[0, :MAIN, lanes]
        o_ref[d, :, CHUNK:] = tail_tile(held_ref[0, MAIN:, lanes].astype(f32)).astype(bf16)
    copy_b.wait()


def push_a_body(d_ref, parts_ref, m_ref, g_ref, x_ref):
    start = pl.multiple_of(d_ref[0] * CHUNK, 128)
    grad = parts_ref[0].astype(f32)
    for r in range(1, N_DP):
        grad += parts_ref[r].astype(f32)
    g_ref[...] = grad.astype(bf16)
    m_main = m_ref[:MAIN, pl.ds(start, CHUNK)]
    m_tail = tail_tile(m_ref[MAIN:, pl.ds(start, CHUNK)])
    moment = decay_rate * jnp.concatenate([m_main, m_tail], axis=1) + grad
    push = (grad + decay_rate * moment).astype(bf16)
    for r in range(N_FSDP):
        x_ref[r] = push


def moment_a_body(i_ref, g0_ref, g1_ref, g2_ref, g3_ref, m_ref, o_ref):
    for k, g_ref in enumerate((g0_ref, g1_ref, g2_ref, g3_ref)):
        for c in range(2):
            start = (((i_ref[0] - k) & 3) * 2 + c) * CHUNK
            lanes = pl.ds(pl.multiple_of(start, 128), CHUNK)
            main = g_ref[c, :, :CHUNK].astype(f32)
            o_ref[:MAIN, lanes] = decay_rate * m_ref[:MAIN, lanes] + main
            tail = g_ref[c, :, CHUNK:].astype(f32)
            for j in range(GROUPS):
                piece = pl.ds(pl.multiple_of(start + 128 * j, 128), 128)
                o_ref[MAIN:, piece] = decay_rate * m_ref[MAIN:, piece] + tail[2 * j : 2 * j + 2]


def half_b_body(c_ref, b_ref, x_ref, o_ref):
    rows = o_ref.shape[0]
    half = b_ref[0, pl.ds(pl.multiple_of(c_ref[0] * rows, rows), rows)]
    o_ref[...] = (half.astype(f32) + x_ref[...].astype(f32)).astype(bf16)


def moment_b_body(d_ref, g_ref, m_ref, o_ref, y_ref, p_ref, scratch):
    grad = g_ref[...].astype(f32)
    moment = decay_rate * m_ref[...] + grad
    o_ref[...] = moment
    y = (grad + decay_rate * moment).astype(bf16)
    y_ref[...] = y
    scratch[...] = lax.dot_general(y, y, (((0,), (0,)), ((), ())), preferred_element_type=f32)
    rows = KV_RANK // N_DP
    p_ref[...] = scratch[pl.ds(pl.multiple_of(d_ref[0] * rows, rows), rows), :].astype(bf16)


def gram_a_body(x_ref, g_ref, full_ref, gram_ref):
    full_ref[: N_FSDP * MAIN] = x_ref[:, :, :CHUNK].reshape(N_FSDP * MAIN, CHUNK)
    tail = x_ref[:, :, CHUNK:].reshape(N_FSDP * MAIN, 128)
    rows = 2 * N_FSDP
    r = lax.broadcasted_iota(jnp.int32, (rows, N_FSDP * MAIN), 0)
    c = lax.broadcasted_iota(jnp.int32, (rows, N_FSDP * MAIN), 1)
    first = MAIN * lax.shift_right_logical(r, 1) + (r & 1)
    for k in range(GROUPS):
        pick = jnp.where(c == first + 2 * k, 1.0, 0.0).astype(bf16)
        full_ref[N_FSDP * MAIN :, 128 * k : 128 * k + 128] = jnp.dot(
            pick, tail, preferred_element_type=f32
        ).astype(bf16)
    x = full_ref[...]
    gram_ref[...] = jnp.zeros_like(gram_ref)
    gram_ref[:KVA_ROWS, :KVA_ROWS] = lax.dot_general(
        x, x, (((1,), (1,)), ((), ())), preferred_element_type=f32
    )
    for i in range(BLOCKS):
        for h in range(2):
            rows = slice(128 * i + 64 * h, 128 * i + 64 * h + 64)
            for j in range(3):
                k = (i + j) % BLOCKS
                g_ref[h, 64 * i : 64 * i + 64, 128 * j : 128 * j + 128] = gram_ref[
                    rows, 128 * k : 128 * k + 128
                ].astype(bf16)


def whole_gram(t_ref, gram_ref):
    for i in range(BLOCKS):
        for j in range(3):
            k = (i + j) % BLOCKS
            block = jnp.concatenate(
                [t_ref[h, 64 * i : 64 * i + 64, 128 * j : 128 * j + 128] for h in range(2)], axis=0
            ).astype(f32)
            gram_ref[128 * i : 128 * i + 128, 128 * k : 128 * k + 128] = block
            if j:
                gram_ref[128 * k : 128 * k + 128, 128 * i : 128 * i + 128] = block.T
    return gram_ref[:KVA_ROWS, :KVA_ROWS]


def mm(a, b):
    return jnp.dot(a.astype(bf16), b.astype(bf16), preferred_element_type=f32)


def gram_scale(gram):
    n = gram.shape[0]
    r = lax.broadcasted_iota(jnp.int32, (n, n), 0)
    c = lax.broadcasted_iota(jnp.int32, (n, n), 1)
    squares = jnp.sum(jnp.where(r == c, gram, 0.0))
    return 1.0 / (jnp.sqrt(squares) + norm_epsilon)


def two_steps(g0):
    d0 = c2 * g0 + c3 * mm(g0, g0)
    t0 = c1 * g0 + mm(d0, g0)
    g1 = c1 * t0 + mm(d0, t0)
    d1 = c2 * g1 + c3 * mm(g1, g1)
    d01 = c1 * (d0 + d1) + mm(d1, d0)
    t1 = c1 * g1 + mm(d1, g1)
    g2 = c1 * t1 + mm(d1, t1)
    return d01, g2


def finish_b_body(i_ref, g0_ref, g1_ref, g2_ref, g3_ref, y_ref, o_ref, gram_ref):
    rows = KV_RANK // 4
    for k, g_ref in enumerate((g0_ref, g1_ref, g2_ref, g3_ref)):
        first = pl.multiple_of(((i_ref[0] - k) & 3) * rows, rows)
        gram_ref[pl.ds(first, rows), :] = g_ref[...].astype(f32)
    gram = gram_ref[...]
    s = gram_scale(gram)
    d01, g2 = two_steps(gram * (s * s))
    d2 = c2 * g2 + c3 * mm(g2, g2)
    rest = c1 * d01 + c1 * c1 * d2 + mm(d2, d01)
    y = y_ref[...]
    total = s * math.sqrt(max(KVB_ROWS, KV_RANK))
    out = (c1 * c1 * c1) * y.astype(f32) + mm(y, rest)
    o_ref[...] = (out * total).astype(bf16)


def finish_a_body(f_ref, g_ref, x_ref, o_ref, gram_ref, d01_ref, g2_ref):
    f = f_ref[0]
    gram = whole_gram(g_ref, gram_ref)
    s = gram_scale(gram)
    d01, g2 = two_steps(gram * (s * s))
    d01_ref[...] = d01
    g2_ref[...] = g2
    main = pl.ds(pl.multiple_of(f * MAIN, MAIN), MAIN)
    base = N_FSDP * MAIN + 8 * lax.shift_right_logical(f, 2)
    tail = pl.ds(pl.multiple_of(base, 8), 8)

    def rows(ref):
        return jnp.concatenate([ref[main, :], ref[tail, :]], axis=0)

    g2_rows = rows(g2_ref)
    d2 = c2 * g2_rows + c3 * mm(g2_rows, g2)
    rest = c1 * rows(d01_ref) + c1 * c1 * d2 + mm(d2, d01)
    x_rows = jnp.concatenate([x_ref[main, :].astype(f32), x_ref[pl.ds(pl.multiple_of(N_FSDP * MAIN + 16 * lax.shift_right_logical(f, 3), 16), 16), :].astype(f32)], axis=0)
    total = s * math.sqrt(max(KVA_ROWS, D))
    moved = mm(rest, x_ref[...])
    out = ((c1 * c1 * c1) * x_rows[:MAIN] + moved[:MAIN]) * total
    o_main = out.astype(bf16)
    q = f & 3
    h = f & 7
    x_tail = x_rows[MAIN : MAIN + 2]
    for j in range(1, 8):
        x_tail = jnp.where(h == j, x_rows[MAIN + 2 * j : MAIN + 2 * j + 2], x_tail)
    m_tail = moved[MAIN : MAIN + 2]
    for j in range(1, 4):
        m_tail = jnp.where(q == j, moved[MAIN + 2 * j : MAIN + 2 * j + 2], m_tail)
    o_tail = tail_tile(((c1 * c1 * c1) * x_tail + m_tail) * total).astype(bf16)
    for r in range(N_DP):
        o_ref[r, :, :CHUNK] = o_main
        o_ref[r, :, CHUNK:] = o_tail


def unpack_body(u_ref, o_ref):
    for d in range(N_DP):
        o_ref[:MAIN, d * CHUNK : (d + 1) * CHUNK] = u_ref[d, :, :CHUNK]
        tail = u_ref[d, :, CHUNK:].astype(f32)
        for k in range(GROUPS):
            piece = slice(d * CHUNK + 128 * k, d * CHUNK + 128 * k + 128)
            o_ref[MAIN:, piece] = tail[2 * k : 2 * k + 2].astype(bf16)


def exchange(x, axis):
    return lax.all_to_all(x, axis, split_axis=0, concat_axis=0, tiled=True)


def total_of(x):
    return jnp.sum(x.astype(f32), axis=0)


def shift(x, axis, n, k):
    return lax.ppermute(x, axis, [(i, (i + k) % n) for i in range(n)])


def others(x, axis, n, step=1):
    return [x] + [shift(x, axis, n, k) for k in range(step, n, step)]


def sum_over(x, axis, n, step=1):
    return pair_sums(others(x, axis, n, step))


def pair_sums(terms):
    terms = [y.astype(f32) for y in terms]
    while len(terms) > 1:
        half = len(terms) // 2
        terms = [terms[k] + terms[k + half] for k in range(half)]
    return terms[0].astype(bf16)


def sum_pair(x, axis, n):
    other = lax.ppermute(x, axis, [(i, i ^ 1) for i in range(n)])
    return (x.astype(f32) + other.astype(f32)).astype(bf16)


def local(kva_parts, kvb_parts, kva_moment, kvb_moment):
    y = lax.axis_index("y").astype(jnp.int32).reshape(1)
    c = lax.axis_index("c").astype(jnp.int32).reshape(1)
    f = lax.axis_index(FSDP).astype(jnp.int32).reshape(1)
    d = y * 2 + c
    rows_b = KV_RANK // N_DP

    half = shape((kvb_parts.shape[1] // 2, KV_RANK), bf16)
    packed, send_b = call(
        pack_body,
        (shape((N_DP, MAIN, WIDE), bf16), half),
        1,
        2,
        [pltpu.VMEM(kva_parts.shape, bf16), pltpu.SemaphoreType.DMA((2,))],
        pl.ANY,
        67_000_000,
    )(c, kva_parts, kvb_parts)
    terms_a = exchange(packed, DP)
    grad_b = call(half_b_body, half, 1, 2)(c, kvb_parts, shift(send_b, "c", 2, 1))
    terms_a, grad_b = lax.optimization_barrier((terms_a, grad_b))
    grads_b = others(grad_b, "y", 4)
    grad_a, push_a = call(
        push_a_body,
        (shape((MAIN, WIDE), bf16), shape((N_FSDP, MAIN, WIDE), bf16)),
        1,
        2,
    )(d, terms_a, kva_moment)
    all_a = exchange(push_a, FSDP)

    grad_b = lax.all_gather(pair_sums(grads_b), "c", tiled=True)
    moment_b, long_b, piece_b = call(
        moment_b_body,
        (
            shape(kvb_moment.shape, f32),
            shape(kvb_moment.shape, bf16),
            shape((rows_b, KV_RANK), bf16),
        ),
        1,
        2,
        [pltpu.VMEM((KV_RANK, KV_RANK), f32)],
        flops=HINT,
    )(d, grad_b, kvb_moment)
    piece_b, grad_a = lax.optimization_barrier((piece_b, grad_a))
    terms_b = others(sum_over(piece_b, "x", 4), "z", 8, 2)

    grads_a = others(lax.all_gather(grad_a, "c"), "y", 4)
    moment_a = call(moment_a_body, shape(kva_moment.shape, f32), 1, 5)(y, *grads_a, kva_moment)
    all_a, moment_a = lax.optimization_barrier((all_a, moment_a))

    gram_a, short_a = call(
        gram_a_body,
        (shape((2, 64 * BLOCKS, 384), bf16), shape((KVA_ROWS, CHUNK), bf16)),
        0,
        1,
        [pltpu.VMEM((128 * BLOCKS, 128 * BLOCKS), f32)],
    )(all_a)
    gram_a = lax.all_gather(gram_a, "c")
    gram_a = lax.dynamic_index_in_dim(gram_a, lax.axis_index("c"), axis=1, keepdims=False)
    gram_a = total_of(gram_a).astype(bf16)
    _, terms_b = lax.optimization_barrier((gram_a, terms_b))
    piece_b = pair_sums(terms_b)
    gram_a = lax.all_gather(sum_over(gram_a, "y", 4), "c")
    piece_b = lax.all_gather(sum_pair(piece_b, "z", 8), "c", tiled=True)

    pieces_b = others(piece_b, "y", 4)
    update_a = call(
        finish_a_body,
        shape((N_DP, MAIN, WIDE), bf16),
        1,
        2,
        [pltpu.VMEM((128 * BLOCKS, 128 * BLOCKS), f32)]
        + [pltpu.VMEM((KVA_ROWS, KVA_ROWS), f32)] * 2,
    )(f, gram_a, short_a)
    update_a, pieces_b = lax.optimization_barrier((update_a, pieces_b))
    update_a = call(unpack_body, shape(kva_moment.shape, bf16))(exchange(update_a, DP))
    update_b = call(
        finish_b_body, shape(long_b.shape, bf16), 1, 5, [pltpu.VMEM((KV_RANK, KV_RANK), f32)]
    )(y, *pieces_b, long_b)
    return (moment_a, moment_b, update_a, update_b)


def solution(mesh):
    fine = Mesh(mesh.devices.reshape(4, 2, 4, 8), DP + FSDP)
    return jax.shard_map(
        local,
        mesh=fine,
        in_specs=(P(DP, FSDP, None), P(DP, FSDP, None), P(FSDP, None), P(FSDP, None)),
        out_specs=(P(FSDP, None), P(FSDP, None), P(FSDP, None), P(FSDP, None)),
        check_vma=False,
    )
```

profile of v0, /device:TPU:1, one launch (start us, length us, event | category | flops | bytes accessed | tf_op | source)
XLA Modules:
  0.0 108.0 jit_solution(4669708321154605081)
XLA Ops:
  0.6 1.9 %shard_map.75 = (bf16[8,16,1024]{2,1,0:T(8,128)(2,1)}, bf16[256,512]{1,0:T(8,128)(2,1)}) custom-call(s32[1]{0:T(128)} %bitcast.1.c_ref, bf16[1,18,7168]{2,1,0:T(8,128)(2,1)} %a_ref.1, bf16[1,512,512]{2,1,0:T(8,128)(2,1)} %b_ref.3), custom_call_target="tpu_custom_call" | custom-call | tf_op jit(solution)/shard_map/pallas_call | solution.py:284
  2.5 0.0 copy-start.1
  2.5 3.3 %collective-permute-start = (bf16[256,512]{1,0:T(8,128)(2,1)}, bf16[256,512]{1,0:T(8,128)(2,1)S(1)}, u32[]{:S(2)}, u32[]{:S(2)}) collective-permute-start(bf16[256,512]{1,0:T(8,128)(2,1)} %get-tuple-element.29), channel_id=1, source_target_pairs={{0,32},{32,0},{1,33},{33,1},{2,34},{34,2},{3,35},{35,3},{4,36},{36... | collective-permute-start | bytes 786440 | tf_op jit(solution)/shard_map/ppermute | solution.py:252
  5.8 3.5 %all-to-all-start = ((bf16[8,16,1024]{2,1,0:T(8,128)(2,1)}), bf16[8,16,1024]{2,1,0:T(8,128)(2,1)S(1)}, u32[]{:S(2)}, u32[]{:S(2)}) async-start(bf16[8,16,1024]{2,1,0:T(8,128)(2,1)} %get-tuple-element.28), calls=%async_computation | async-start | bytes 524288 | tf_op jit(solution)/shard_map/all_to_all | solution.py:244
  9.4 0.1 shard_map.76
  9.4 6.4 %all-to-all-done.parts_ref = bf16[8,16,1024]{2,1,0:T(8,128)(2,1)S(1)} async-done(((bf16[8,16,1024]{2,1,0:T(8,128)(2,1)}), bf16[8,16,1024]{2,1,0:T(8,128)(2,1)S(1)}, u32[]{:S(2)}, u32[]{:S(2)}) %all-to-all-start) | async-done | bytes 262176 | tf_op jit(solution)/shard_map/all_to_all | solution.py:244
  15.8 0.9 collective-permute-start.3
  16.7 0.6 collective-permute-start.2
  17.3 0.6 collective-permute-start.1
  17.9 1.1 %shard_map.77 = (bf16[16,1024]{1,0:T(8,128)(2,1)S(1)}, bf16[32,16,1024]{2,1,0:T(8,128)(2,1)}) custom-call(s32[1]{0:T(128)S(6)} %add.49.d_ref, bf16[8,16,1024]{2,1,0:T(8,128)(2,1)S(1)} %all-to-all-done.parts_ref, f32[18,7168]{1,0:T(8,128)S(1)} %copy-done), custom_call_target="tpu_custom_call" | custom-call | tf_op jit(solution)/shard_map/pallas_call | solution.py:297
  19.1 10.5 %all-to-all-start.1 = ((bf16[32,16,1024]{2,1,0:T(8,128)(2,1)}), bf16[32,16,1024]{2,1,0:T(8,128)(2,1)S(1)}, u32[]{:S(2)}, u32[]{:S(2)}) async-start(bf16[32,16,1024]{2,1,0:T(8,128)(2,1)} %get-tuple-element.31), calls=%async_computation.1 | async-start | bytes 2097152 | tf_op jit(solution)/shard_map/all_to_all | solution.py:244
  29.6 0.0 copy-start.2
  29.6 0.0 collective-permute-done.2
  29.6 0.1 add_convert_fusion
  29.8 4.5 %all_gather.24.g_ref = bf16[512,512]{1,0:T(8,128)(2,1)S(1)} all-gather(bf16[256,512]{1,0:T(8,128)(2,1)S(1)} %add_convert_fusion), channel_id=1, replica_groups=mesh['y'=4,'c'=2,'x'=4,'z'=8] {'c'}, dimensions={0}, use_global_device_ids=true | all-gather | bytes 786432 | tf_op jit(solution)/shard_map/all_gather | solution.py:305
  34.2 1.2 %shard_map.78 = (f32[512,512]{1,0:T(8,128)}, bf16[512,512]{1,0:T(8,128)(2,1)S(1)}, bf16[64,512]{1,0:T(8,128)(2,1)S(1)}) custom-call(s32[1]{0:T(128)S(6)} %add.49.d_ref, bf16[512,512]{1,0:T(8,128)(2,1)S(1)} %all_gather.24.g_ref, f32[512,512]{1,0:T(8,128)S(1)} %copy-done.2), custom_call_target="tpu_custom_call" | custom-call | flops 40000000000 | tf_op jit(solution)/shard_map/pallas_call | solution.py:306
  35.4 2.1 %collective-permute-start.12 = (bf16[64,512]{1,0:T(8,128)(2,1)S(1)}, bf16[64,512]{1,0:T(8,128)(2,1)S(1)}, u32[]{:S(2)}, u32[]{:S(2)}) collective-permute-start(bf16[64,512]{1,0:T(8,128)(2,1)S(1)} %get-tuple-element.41), channel_id=1, source_target_pairs={{0,24},{8,0},{16,8},{24,16},{1,25},{9,1},{17,9},{25,17},{2,26},{10... | collective-permute-start | bytes 196616 | tf_op jit(solution)/shard_map/ppermute | solution.py:252
  37.6 1.7 %collective-permute-start.10 = (bf16[64,512]{1,0:T(8,128)(2,1)S(1)}, bf16[64,512]{1,0:T(8,128)(2,1)S(1)}, u32[]{:S(2)}, u32[]{:S(2)}) collective-permute-start(bf16[64,512]{1,0:T(8,128)(2,1)S(1)} %get-tuple-element.41), channel_id=1, source_target_pairs={{0,16},{8,24},{16,0},{24,8},{1,17},{9,25},{17,1},{25,9},{2,18},{10... | collective-permute-start | bytes 196616 | tf_op jit(solution)/shard_map/ppermute | solution.py:252
  39.3 2.7 %all-gather = bf16[32,1024]{1,0:T(8,128)(2,1)S(1)} all-gather(bf16[16,1024]{1,0:T(8,128)(2,1)S(1)} %get-tuple-element.35), channel_id=2, replica_groups=mesh['y'=4,'c'=2,'x'=4,'z'=8] {'c'}, dimensions={0}, use_global_device_ids=true | all-gather | bytes 98304 | tf_op jit(solution)/shard_map/all_gather | solution.py:321
  42.0 2.3 %collective-permute-start.4 = (bf16[2,16,1024]{2,1,0:T(8,128)(2,1)S(1)}, bf16[2,16,1024]{2,1,0:T(8,128)(2,1)S(1)}, u32[]{:S(2)}, u32[]{:S(2)}) collective-permute-start(bf16[2,16,1024]{2,1,0:T(8,128)(2,1)S(1)} %bitcast.7), channel_id=1, source_target_pairs={{0,64},{64,128},{128,192},{192,0},{1,65},{65,129},{129,193},{193,1... | collective-permute-start | bytes 196616 | tf_op jit(solution)/shard_map/ppermute | solution.py:252
  44.3 1.2 %collective-permute-start.5 = (bf16[2,16,1024]{2,1,0:T(8,128)(2,1)S(1)}, bf16[2,16,1024]{2,1,0:T(8,128)(2,1)S(1)}, u32[]{:S(2)}, u32[]{:S(2)}) collective-permute-start(bf16[2,16,1024]{2,1,0:T(8,128)(2,1)S(1)} %bitcast.8), channel_id=1, source_target_pairs={{0,128},{64,192},{128,0},{192,64},{1,129},{65,193},{129,1},{193,65... | collective-permute-start | bytes 196616 | tf_op jit(solution)/shard_map/ppermute | solution.py:252
  45.5 0.0 collective-permute-done.12
  45.5 1.2 %collective-permute-start.6 = (bf16[2,16,1024]{2,1,0:T(8,128)(2,1)S(1)}, bf16[2,16,1024]{2,1,0:T(8,128)(2,1)S(1)}, u32[]{:S(2)}, u32[]{:S(2)}) collective-permute-start(bf16[2,16,1024]{2,1,0:T(8,128)(2,1)S(1)} %bitcast.9), channel_id=1, source_target_pairs={{0,192},{64,0},{128,64},{192,128},{1,193},{65,1},{129,65},{193,129... | collective-permute-start | bytes 196616 | tf_op jit(solution)/shard_map/ppermute | solution.py:252
  46.8 2.2 %collective-permute-start.13 = (bf16[64,512]{1,0:T(8,128)(2,1)S(1)}, bf16[64,512]{1,0:T(8,128)(2,1)S(1)}, u32[]{:S(2)}, u32[]{:S(2)}) collective-permute-start(bf16[64,512]{1,0:T(8,128)(2,1)S(1)} %add_convert_fusion.4), channel_id=1, source_target_pairs={{0,2},{1,3},{2,4},{3,5},{4,6},{5,7},{6,0},{7,1},{8,10},{9,11},{10,... | collective-permute-start | bytes 196616 | tf_op jit(solution)/shard_map/ppermute | solution.py:252
  48.9 5.3 %collective-permute-start.14 = (bf16[64,512]{1,0:T(8,128)(2,1)S(1)}, bf16[64,512]{1,0:T(8,128)(2,1)S(1)}, u32[]{:S(2)}, u32[]{:S(2)}) collective-permute-start(bf16[64,512]{1,0:T(8,128)(2,1)S(1)} %add_convert_fusion.4), channel_id=1, source_target_pairs={{0,4},{1,5},{2,6},{3,7},{4,0},{5,1},{6,2},{7,3},{8,12},{9,13},{10,... | collective-permute-start | bytes 196616 | tf_op jit(solution)/shard_map/ppermute | solution.py:252
  54.2 1.3 %collective-permute-start.15 = (bf16[64,512]{1,0:T(8,128)(2,1)S(1)}, bf16[64,512]{1,0:T(8,128)(2,1)S(1)}, u32[]{:S(2)}, u32[]{:S(2)}) collective-permute-start(bf16[64,512]{1,0:T(8,128)(2,1)S(1)} %add_convert_fusion.4), channel_id=1, source_target_pairs={{0,6},{1,7},{2,0},{3,1},{4,2},{5,3},{6,4},{7,5},{8,14},{9,15},{10,... | collective-permute-start | bytes 196616 | tf_op jit(solution)/shard_map/ppermute | solution.py:252
  55.5 1.0 shard_map.79
  56.5 0.0 all-to-all-done.1.x_ref
  56.5 1.3 %shard_map.80 = (bf16[2,320,384]{2,1,0:T(8,128)(2,1)S(1)}, bf16[576,896]{1,0:T(8,128)(2,1)S(1)}) custom-call(bf16[32,16,1024]{2,1,0:T(8,128)(2,1)S(1)} %all-to-all-done.1.x_ref), custom_call_target="tpu_custom_call" | custom-call | tf_op jit(solution)/shard_map/pallas_call | solution.py:325
  57.8 6.0 %all-gather.1 = bf16[4,320,384]{2,1,0:T(8,128)(2,1)S(1)} all-gather(bf16[2,320,384]{2,1,0:T(8,128)(2,1)S(1)} %get-tuple-element.39), channel_id=3, replica_groups=mesh['y'=4,'c'=2,'x'=4,'z'=8] {'c'}, dimensions={0}, use_global_device_ids=true | all-gather | bytes 1474560 | tf_op jit(solution)/shard_map/all_gather | solution.py:332
  63.8 0.1 dynamic-slice_reduce_fusion
  63.8 0.0 collective-permute-done.14
  63.9 3.0 %collective-permute-start.16 = (bf16[64,512]{1,0:T(8,128)(2,1)S(1)}, bf16[64,512]{1,0:T(8,128)(2,1)S(1)}, u32[]{:S(2)}, u32[]{:S(2)}) collective-permute-start(bf16[64,512]{1,0:T(8,128)(2,1)S(1)} %add_convert_fusion.3), channel_id=1, source_target_pairs={{0,1},{1,0},{2,3},{3,2},{4,5},{5,4},{6,7},{7,6},{8,9},{9,8},{10,11... | collective-permute-start | bytes 196616 | tf_op jit(solution)/shard_map/ppermute | solution.py:272
  66.9 4.0 %collective-permute-start.9 = (bf16[320,384]{1,0:T(8,128)(2,1)S(1)}, bf16[320,384]{1,0:T(8,128)(2,1)S(1)}, u32[]{:S(2)}, u32[]{:S(2)}) collective-permute-start(bf16[320,384]{1,0:T(8,128)(2,1)S(1)} %dynamic-slice_reduce_fusion), channel_id=1, source_target_pairs={{0,192},{64,0},{128,64},{192,128},{1,193},{65,1},{129,65},{193,129... | collective-permute-start | bytes 737288 | tf_op jit(solution)/shard_map/ppermute | solution.py:252
  70.9 0.1 collective-permute-start.8
  70.9 1.8 %collective-permute-start.7 = (bf16[320,384]{1,0:T(8,128)(2,1)S(1)}, bf16[320,384]{1,0:T(8,128)(2,1)S(1)}, u32[]{:S(2)}, u32[]{:S(2)}) collective-permute-start(bf16[320,384]{1,0:T(8,128)(2,1)S(1)} %dynamic-slice_reduce_fusion), channel_id=1, source_target_pairs={{0,128},{64,192},{128,0},{192,64},{1,129},{65,193},{129,1},{193,65... | collective-permute-start | bytes 737288 | tf_op jit(solution)/shard_map/ppermute | solution.py:252
  72.7 2.8 %all_gather.31.g0_ref = bf16[128,512]{1,0:T(8,128)(2,1)S(1)} all-gather(bf16[64,512]{1,0:T(8,128)(2,1)S(1)} %add_convert_fusion.2), channel_id=1, replica_groups=mesh['y'=4,'c'=2,'x'=4,'z'=8] {'c'}, dimensions={0}, use_global_device_ids=true | all-gather | bytes 196608 | tf_op jit(solution)/shard_map/all_gather | solution.py:338
  75.5 1.7 %collective-permute-start.17 = (bf16[128,512]{1,0:T(8,128)(2,1)S(1)}, bf16[128,512]{1,0:T(8,128)(2,1)S(1)}, u32[]{:S(2)}, u32[]{:S(2)}) collective-permute-start(bf16[128,512]{1,0:T(8,128)(2,1)S(1)} %all_gather.31.g0_ref), channel_id=1, source_target_pairs={{0,64},{64,128},{128,192},{192,0},{1,65},{65,129},{129,193},{193,1... | collective-permute-start | bytes 393224 | tf_op jit(solution)/shard_map/ppermute | solution.py:252
  77.2 1.8 %collective-permute-start.18 = (bf16[128,512]{1,0:T(8,128)(2,1)S(1)}, bf16[128,512]{1,0:T(8,128)(2,1)S(1)}, u32[]{:S(2)}, u32[]{:S(2)}) collective-permute-start(bf16[128,512]{1,0:T(8,128)(2,1)S(1)} %all_gather.31.g0_ref), channel_id=1, source_target_pairs={{0,128},{64,192},{128,0},{192,64},{1,129},{65,193},{129,1},{193,65... | collective-permute-start | bytes 393224 | tf_op jit(solution)/shard_map/ppermute | solution.py:252
  79.0 0.5 collective-permute-start.19
  79.6 3.8 %collective-permute-done.7 = bf16[320,384]{1,0:T(8,128)(2,1)S(1)} collective-permute-done((bf16[320,384]{1,0:T(8,128)(2,1)S(1)}, bf16[320,384]{1,0:T(8,128)(2,1)S(1)}, u32[]{:S(2)}, u32[]{:S(2)}) %collective-permute-start.7) | collective-permute-done | bytes 245792 | tf_op jit(solution)/shard_map/ppermute | solution.py:252
  83.4 0.1 add_convert_fusion.1
  83.5 6.7 %all-gather.2 = bf16[640,384]{1,0:T(8,128)(2,1)S(1)} all-gather(bf16[320,384]{1,0:T(8,128)(2,1)S(1)} %add_convert_fusion.1), channel_id=4, replica_groups=mesh['y'=4,'c'=2,'x'=4,'z'=8] {'c'}, dimensions={0}, use_global_device_ids=true | all-gather | bytes 737280 | tf_op jit(solution)/shard_map/all_gather | solution.py:337
  90.2 6.6 %shard_map.81 = bf16[8,16,1024]{2,1,0:T(8,128)(2,1)} custom-call(s32[1]{0:T(128)} %bitcast.3.f_ref, bf16[2,320,384]{2,1,0:T(8,128)(2,1)S(1)} %bitcast.6, bf16[576,896]{1,0:T(8,128)(2,1)S(1)} %get-tuple-element.40.x_ref), custom_call_target="tpu_custom_call" | custom-call | tf_op jit(solution)/shard_map/pallas_call | solution.py:341
  96.9 3.9 %all-to-all-start.2 = ((bf16[8,16,1024]{2,1,0:T(8,128)(2,1)}), bf16[8,16,1024]{2,1,0:T(8,128)(2,1)S(1)}, u32[]{:S(2)}, u32[]{:S(2)}) async-start(bf16[8,16,1024]{2,1,0:T(8,128)(2,1)} %shard_map.81), calls=%async_computation.2 | async-start | bytes 524288 | tf_op jit(solution)/shard_map/all_to_all | solution.py:244
  100.7 4.5 %shard_map.83 = bf16[512,512]{1,0:T(8,128)(2,1)} custom-call(s32[1]{0:T(128)} %bitcast.i_ref, bf16[128,512]{1,0:T(8,128)(2,1)S(1)} %all_gather.31.g0_ref, bf16[128,512]{1,0:T(8,128)(2,1)S(1)} %collective-permute-done.17.g1_ref, bf16[128,512]{1,0:T(8,128)(2,1)S(1)} %collective-permute-done.18.g2_ref, bf16[128,512]{1,0:T(8,128)(2,1)S(1)} %collective-permute-done.19.g3_ref, ...), custom_call_target="tpu_custom_call" | custom-call | tf_op jit(solution)/shard_map/pallas_call | solution.py:351
  105.2 2.0 %all-to-all-done.2.u_ref = bf16[8,16,1024]{2,1,0:T(8,128)(2,1)S(1)} async-done(((bf16[8,16,1024]{2,1,0:T(8,128)(2,1)}), bf16[8,16,1024]{2,1,0:T(8,128)(2,1)S(1)}, u32[]{:S(2)}, u32[]{:S(2)}) %all-to-all-start.2) | async-done | bytes 262176 | tf_op jit(solution)/shard_map/all_to_all | solution.py:244
  107.2 0.8 shard_map.82
  (24 shorter events, 0.1 us)
Async XLA Ops:
  2.5 6.9 %copy-start.1 = (bf16[1,512,512]{2,1,0:T(8,128)(2,1)S(1)}, bf16[1,512,512]{2,1,0:T(8,128)(2,1)}, u32[]{:S(2)}) copy-start(bf16[1,512,512]{2,1,0:T(8,128)(2,1)} %b_ref.3) | copy-start | bytes 1572868
  2.5 6.8 %collective-permute-start = (bf16[256,512]{1,0:T(8,128)(2,1)}, bf16[256,512]{1,0:T(8,128)(2,1)S(1)}, u32[]{:S(2)}, u32[]{:S(2)}) collective-permute-start(bf16[256,512]{1,0:T(8,128)(2,1)} %get-tuple-element.29), channel_id=1, source_target_pairs={{0,32},{32,0},{1,33},{33,1},{2,34},{34,2},{3,35},{35,3},{4,36},{36... | collective-permute-start | bytes 786440 | tf_op jit(solution)/shard_map/ppermute | solution.py:252
  5.8 12.1 %copy-start = (f32[18,7168]{1,0:T(8,128)S(1)}, f32[18,7168]{1,0:T(8,128)}, u32[]{:S(2)}) copy-start(f32[18,7168]{1,0:T(8,128)} %m_ref.5) | copy-start | bytes 1548292
  5.8 10.0 %all-to-all-start = ((bf16[8,16,1024]{2,1,0:T(8,128)(2,1)}), bf16[8,16,1024]{2,1,0:T(8,128)(2,1)S(1)}, u32[]{:S(2)}, u32[]{:S(2)}) async-start(bf16[8,16,1024]{2,1,0:T(8,128)(2,1)} %get-tuple-element.28), calls=%async_computation | async-start | bytes 524288 | tf_op jit(solution)/shard_map/all_to_all | solution.py:244
  15.8 13.7 %collective-permute-start.3 = (bf16[256,512]{1,0:T(8,128)(2,1)S(1)}, bf16[256,512]{1,0:T(8,128)(2,1)S(1)}, u32[]{:S(2)}, u32[]{:S(2)}) collective-permute-start(bf16[256,512]{1,0:T(8,128)(2,1)S(1)} %shard_map.76), channel_id=1, source_target_pairs={{0,192},{64,0},{128,64},{192,128},{1,193},{65,1},{129,65},{193,129... | collective-permute-start | bytes 786440 | tf_op jit(solution)/shard_map/ppermute | solution.py:252
  16.7 12.9 %collective-permute-start.2 = (bf16[256,512]{1,0:T(8,128)(2,1)S(1)}, bf16[256,512]{1,0:T(8,128)(2,1)S(1)}, u32[]{:S(2)}, u32[]{:S(2)}) collective-permute-start(bf16[256,512]{1,0:T(8,128)(2,1)S(1)} %shard_map.76), channel_id=1, source_target_pairs={{0,64},{64,128},{128,192},{192,0},{1,65},{65,129},{129,193},{193,1... | collective-permute-start | bytes 786440 | tf_op jit(solution)/shard_map/ppermute | solution.py:252
  17.3 12.3 %collective-permute-start.1 = (bf16[256,512]{1,0:T(8,128)(2,1)S(1)}, bf16[256,512]{1,0:T(8,128)(2,1)S(1)}, u32[]{:S(2)}, u32[]{:S(2)}) collective-permute-start(bf16[256,512]{1,0:T(8,128)(2,1)S(1)} %shard_map.76), channel_id=1, source_target_pairs={{0,128},{64,192},{128,0},{192,64},{1,129},{65,193},{129,1},{193,65... | collective-permute-start | bytes 786440 | tf_op jit(solution)/shard_map/ppermute | solution.py:252
  19.1 37.4 %all-to-all-start.1 = ((bf16[32,16,1024]{2,1,0:T(8,128)(2,1)}), bf16[32,16,1024]{2,1,0:T(8,128)(2,1)S(1)}, u32[]{:S(2)}, u32[]{:S(2)}) async-start(bf16[32,16,1024]{2,1,0:T(8,128)(2,1)} %get-tuple-element.31), calls=%async_computation.1 | async-start | bytes 2097152 | tf_op jit(solution)/shard_map/all_to_all | solution.py:244
  29.6 4.6 %copy-start.2 = (f32[512,512]{1,0:T(8,128)S(1)}, f32[512,512]{1,0:T(8,128)}, u32[]{:S(2)}) copy-start(f32[512,512]{1,0:T(8,128)} %m_ref.4) | copy-start | bytes 3145732
  35.4 10.1 %collective-permute-start.12 = (bf16[64,512]{1,0:T(8,128)(2,1)S(1)}, bf16[64,512]{1,0:T(8,128)(2,1)S(1)}, u32[]{:S(2)}, u32[]{:S(2)}) collective-permute-start(bf16[64,512]{1,0:T(8,128)(2,1)S(1)} %get-tuple-element.41), channel_id=1, source_target_pairs={{0,24},{8,0},{16,8},{24,16},{1,25},{9,1},{17,9},{25,17},{2,26},{10... | collective-permute-start | bytes 196616 | tf_op jit(solution)/shard_map/ppermute | solution.py:252
  37.6 9.2 %collective-permute-start.11 = (bf16[64,512]{1,0:T(8,128)(2,1)S(1)}, bf16[64,512]{1,0:T(8,128)(2,1)S(1)}, u32[]{:S(2)}, u32[]{:S(2)}) collective-permute-start(bf16[64,512]{1,0:T(8,128)(2,1)S(1)} %get-tuple-element.41), channel_id=1, source_target_pairs={{0,8},{8,16},{16,24},{24,0},{1,9},{9,17},{17,25},{25,1},{2,10},{10... | collective-permute-start | bytes 196616 | tf_op jit(solution)/shard_map/ppermute | solution.py:252
  37.6 9.2 %collective-permute-start.10 = (bf16[64,512]{1,0:T(8,128)(2,1)S(1)}, bf16[64,512]{1,0:T(8,128)(2,1)S(1)}, u32[]{:S(2)}, u32[]{:S(2)}) collective-permute-start(bf16[64,512]{1,0:T(8,128)(2,1)S(1)} %get-tuple-element.41), channel_id=1, source_target_pairs={{0,16},{8,24},{16,0},{24,8},{1,17},{9,25},{17,1},{25,9},{2,18},{10... | collective-permute-start | bytes 196616 | tf_op jit(solution)/shard_map/ppermute | solution.py:252
  42.0 12.2 %collective-permute-start.4 = (bf16[2,16,1024]{2,1,0:T(8,128)(2,1)S(1)}, bf16[2,16,1024]{2,1,0:T(8,128)(2,1)S(1)}, u32[]{:S(2)}, u32[]{:S(2)}) collective-permute-start(bf16[2,16,1024]{2,1,0:T(8,128)(2,1)S(1)} %bitcast.7), channel_id=1, source_target_pairs={{0,64},{64,128},{128,192},{192,0},{1,65},{65,129},{129,193},{193,1... | collective-permute-start | bytes 196616 | tf_op jit(solution)/shard_map/ppermute | solution.py:252
  44.3 11.2 %collective-permute-start.5 = (bf16[2,16,1024]{2,1,0:T(8,128)(2,1)S(1)}, bf16[2,16,1024]{2,1,0:T(8,128)(2,1)S(1)}, u32[]{:S(2)}, u32[]{:S(2)}) collective-permute-start(bf16[2,16,1024]{2,1,0:T(8,128)(2,1)S(1)} %bitcast.8), channel_id=1, source_target_pairs={{0,128},{64,192},{128,0},{192,64},{1,129},{65,193},{129,1},{193,65... | collective-permute-start | bytes 196616 | tf_op jit(solution)/shard_map/ppermute | solution.py:252
  45.5 10.0 %collective-permute-start.6 = (bf16[2,16,1024]{2,1,0:T(8,128)(2,1)S(1)}, bf16[2,16,1024]{2,1,0:T(8,128)(2,1)S(1)}, u32[]{:S(2)}, u32[]{:S(2)}) collective-permute-start(bf16[2,16,1024]{2,1,0:T(8,128)(2,1)S(1)} %bitcast.9), channel_id=1, source_target_pairs={{0,192},{64,0},{128,64},{192,128},{1,193},{65,1},{129,65},{193,129... | collective-permute-start | bytes 196616 | tf_op jit(solution)/shard_map/ppermute | solution.py:252
  46.8 17.0 %collective-permute-start.13 = (bf16[64,512]{1,0:T(8,128)(2,1)S(1)}, bf16[64,512]{1,0:T(8,128)(2,1)S(1)}, u32[]{:S(2)}, u32[]{:S(2)}) collective-permute-start(bf16[64,512]{1,0:T(8,128)(2,1)S(1)} %add_convert_fusion.4), channel_id=1, source_target_pairs={{0,2},{1,3},{2,4},{3,5},{4,6},{5,7},{6,0},{7,1},{8,10},{9,11},{10,... | collective-permute-start | bytes 196616 | tf_op jit(solution)/shard_map/ppermute | solution.py:252
  48.9 14.9 %collective-permute-start.14 = (bf16[64,512]{1,0:T(8,128)(2,1)S(1)}, bf16[64,512]{1,0:T(8,128)(2,1)S(1)}, u32[]{:S(2)}, u32[]{:S(2)}) collective-permute-start(bf16[64,512]{1,0:T(8,128)(2,1)S(1)} %add_convert_fusion.4), channel_id=1, source_target_pairs={{0,4},{1,5},{2,6},{3,7},{4,0},{5,1},{6,2},{7,3},{8,12},{9,13},{10,... | collective-permute-start | bytes 196616 | tf_op jit(solution)/shard_map/ppermute | solution.py:252
  54.2 9.6 %collective-permute-start.15 = (bf16[64,512]{1,0:T(8,128)(2,1)S(1)}, bf16[64,512]{1,0:T(8,128)(2,1)S(1)}, u32[]{:S(2)}, u32[]{:S(2)}) collective-permute-start(bf16[64,512]{1,0:T(8,128)(2,1)S(1)} %add_convert_fusion.4), channel_id=1, source_target_pairs={{0,6},{1,7},{2,0},{3,1},{4,2},{5,3},{6,4},{7,5},{8,14},{9,15},{10,... | collective-permute-start | bytes 196616 | tf_op jit(solution)/shard_map/ppermute | solution.py:252
  63.9 8.8 %collective-permute-start.16 = (bf16[64,512]{1,0:T(8,128)(2,1)S(1)}, bf16[64,512]{1,0:T(8,128)(2,1)S(1)}, u32[]{:S(2)}, u32[]{:S(2)}) collective-permute-start(bf16[64,512]{1,0:T(8,128)(2,1)S(1)} %add_convert_fusion.3), channel_id=1, source_target_pairs={{0,1},{1,0},{2,3},{3,2},{4,5},{5,4},{6,7},{7,6},{8,9},{9,8},{10,11... | collective-permute-start | bytes 196616 | tf_op jit(solution)/shard_map/ppermute | solution.py:272
  66.9 12.1 %collective-permute-start.9 = (bf16[320,384]{1,0:T(8,128)(2,1)S(1)}, bf16[320,384]{1,0:T(8,128)(2,1)S(1)}, u32[]{:S(2)}, u32[]{:S(2)}) collective-permute-start(bf16[320,384]{1,0:T(8,128)(2,1)S(1)} %dynamic-slice_reduce_fusion), channel_id=1, source_target_pairs={{0,192},{64,0},{128,64},{192,128},{1,193},{65,1},{129,65},{193,129... | collective-permute-start | bytes 737288 | tf_op jit(solution)/shard_map/ppermute | solution.py:252
  70.9 8.7 %collective-permute-start.8 = (bf16[320,384]{1,0:T(8,128)(2,1)S(1)}, bf16[320,384]{1,0:T(8,128)(2,1)S(1)}, u32[]{:S(2)}, u32[]{:S(2)}) collective-permute-start(bf16[320,384]{1,0:T(8,128)(2,1)S(1)} %dynamic-slice_reduce_fusion), channel_id=1, source_target_pairs={{0,64},{64,128},{128,192},{192,0},{1,65},{65,129},{129,193},{193,1... | collective-permute-start | bytes 737288 | tf_op jit(solution)/shard_map/ppermute | solution.py:252
  70.9 12.5 %collective-permute-start.7 = (bf16[320,384]{1,0:T(8,128)(2,1)S(1)}, bf16[320,384]{1,0:T(8,128)(2,1)S(1)}, u32[]{:S(2)}, u32[]{:S(2)}) collective-permute-start(bf16[320,384]{1,0:T(8,128)(2,1)S(1)} %dynamic-slice_reduce_fusion), channel_id=1, source_target_pairs={{0,128},{64,192},{128,0},{192,64},{1,129},{65,193},{129,1},{193,65... | collective-permute-start | bytes 737288 | tf_op jit(solution)/shard_map/ppermute | solution.py:252
  75.5 21.3 %collective-permute-start.17 = (bf16[128,512]{1,0:T(8,128)(2,1)S(1)}, bf16[128,512]{1,0:T(8,128)(2,1)S(1)}, u32[]{:S(2)}, u32[]{:S(2)}) collective-permute-start(bf16[128,512]{1,0:T(8,128)(2,1)S(1)} %all_gather.31.g0_ref), channel_id=1, source_target_pairs={{0,64},{64,128},{128,192},{192,0},{1,65},{65,129},{129,193},{193,1... | collective-permute-start | bytes 393224 | tf_op jit(solution)/shard_map/ppermute | solution.py:252
  77.2 19.7 %collective-permute-start.18 = (bf16[128,512]{1,0:T(8,128)(2,1)S(1)}, bf16[128,512]{1,0:T(8,128)(2,1)S(1)}, u32[]{:S(2)}, u32[]{:S(2)}) collective-permute-start(bf16[128,512]{1,0:T(8,128)(2,1)S(1)} %all_gather.31.g0_ref), channel_id=1, source_target_pairs={{0,128},{64,192},{128,0},{192,64},{1,129},{65,193},{129,1},{193,65... | collective-permute-start | bytes 393224 | tf_op jit(solution)/shard_map/ppermute | solution.py:252
  79.0 17.8 %collective-permute-start.19 = (bf16[128,512]{1,0:T(8,128)(2,1)S(1)}, bf16[128,512]{1,0:T(8,128)(2,1)S(1)}, u32[]{:S(2)}, u32[]{:S(2)}) collective-permute-start(bf16[128,512]{1,0:T(8,128)(2,1)S(1)} %all_gather.31.g0_ref), channel_id=1, source_target_pairs={{0,192},{64,0},{128,64},{192,128},{1,193},{65,1},{129,65},{193,129... | collective-permute-start | bytes 393224 | tf_op jit(solution)/shard_map/ppermute | solution.py:252
  96.9 10.4 %all-to-all-start.2 = ((bf16[8,16,1024]{2,1,0:T(8,128)(2,1)}), bf16[8,16,1024]{2,1,0:T(8,128)(2,1)S(1)}, u32[]{:S(2)}, u32[]{:S(2)}) async-start(bf16[8,16,1024]{2,1,0:T(8,128)(2,1)} %shard_map.81), calls=%async_computation.2 | async-start | bytes 524288 | tf_op jit(solution)/shard_map/all_to_all | solution.py:244
where the time goes:
time: 108 us
  starting transfers between devices  53.5 us (50%)
  blocking collectives  22.6 us (21%)
  Pallas kernels  18.4 us (17%)
  waiting for transfers between devices  12.3 us (11%)
    ppermute x19, starting transfers between devices, shift(): return lax.ppermute(x, axis, [(i, (i + k) % n) for i in range(n)])  32.7 us
    all_to_all x3, starting transfers between devices, exchange(): return lax.all_to_all(x, axis, split_axis=0, concat_axis=0, tiled=True)  17.9 us
    all_to_all x3, waiting for transfers between devices, exchange(): return lax.all_to_all(x, axis, split_axis=0, concat_axis=0, tiled=True)  8.44 us
    all_gather x1, blocking collectives, local(): gram_a = lax.all_gather(sum_over(gram_a, 'y', 4), 'c')  6.66 us
    pallas_call x1, Pallas kernels, local(): call(finish_a_body, shape((N_DP, MAIN, WIDE), bf16), 1, 2, [pltpu.VMEM((1...  6.64 us
    all_gather x1, blocking collectives, local(): gram_a = lax.all_gather(gram_a, 'c')  5.97 us
    pallas_call x1, Pallas kernels, local(): call(finish_b_body, shape(long_b.shape, bf16), 1, 5, [pltpu.VMEM((KV_RANK...  4.47 us
    all_gather x1, blocking collectives, local(): grad_b = lax.all_gather(pair_sums(grads_b), 'c', tiled=True)  4.46 us
  transfers between devices with their start and end apart: 23, of which 3 were waited for; matrix products, arithmetic and copies ran while one was open for 0% of the time, Pallas kernels for 15%

commit v1 on v0

--- a/solution.py
+++ b/solution.py
@@ -77,12 +77,13 @@
     grad = parts_ref[0].astype(f32)
     for r in range(1, N_DP):
         grad += parts_ref[r].astype(f32)
-    g_ref[...] = grad.astype(bf16)
+    g_ref[:MAIN] = grad[:, :KV_RANK].astype(bf16)
+    g_ref[MAIN:] = grad[:, KV_RANK:].astype(bf16)
     m_main = m_ref[:MAIN, pl.ds(start, CHUNK)]
     m_tail = tail_tile(m_ref[MAIN:, pl.ds(start, CHUNK)])
     moment = decay_rate * jnp.concatenate([m_main, m_tail], axis=1) + grad
     push = (grad + decay_rate * moment).astype(bf16)
-    for r in range(N_FSDP):
+    for r in range(x_ref.shape[0]):
         x_ref[r] = push
 
 
@@ -91,9 +92,10 @@
         for c in range(2):
             start = (((i_ref[0] - k) & 3) * 2 + c) * CHUNK
             lanes = pl.ds(pl.multiple_of(start, 128), CHUNK)
-            main = g_ref[c, :, :CHUNK].astype(f32)
+            grad = jnp.concatenate([g_ref[c, :MAIN], g_ref[c, MAIN:]], axis=1).astype(f32)
+            main = grad[:, :CHUNK]
             o_ref[:MAIN, lanes] = decay_rate * m_ref[:MAIN, lanes] + main
-            tail = g_ref[c, :, CHUNK:].astype(f32)
+            tail = grad[:, CHUNK:]
             for j in range(GROUPS):
                 piece = pl.ds(pl.multiple_of(start + 128 * j, 128), 128)
                 o_ref[MAIN:, piece] = decay_rate * m_ref[MAIN:, piece] + tail[2 * j : 2 * j + 2]
@@ -105,8 +107,18 @@
     o_ref[...] = (half.astype(f32) + x_ref[...].astype(f32)).astype(bf16)
 
 
-def moment_b_body(d_ref, g_ref, m_ref, o_ref, y_ref, p_ref, scratch):
-    grad = g_ref[...].astype(f32)
+def sum_b_body(b0_ref, b1_ref, b2_ref, b3_ref, g_ref, o_ref):
+    rows = b0_ref.shape[0]
+    first = b0_ref[...].astype(f32) + b2_ref[...].astype(f32)
+    second = b1_ref[...].astype(f32) + b3_ref[...].astype(f32)
+    o_ref[:rows] = (first + second).astype(bf16)
+    o_ref[rows:] = g_ref[...]
+
+
+def moment_b_body(d_ref, g_ref, m_ref, o_ref, y_ref, p_ref, a_ref, scratch):
+    rows = m_ref.shape[0] // 2
+    a_ref[...] = g_ref[:, rows:]
+    grad = jnp.concatenate([g_ref[0, :rows], g_ref[1, :rows]], axis=0).astype(f32)
     moment = decay_rate * m_ref[...] + grad
     o_ref[...] = moment
     y = (grad + decay_rate * moment).astype(bf16)
@@ -116,9 +128,12 @@
     p_ref[...] = scratch[pl.ds(pl.multiple_of(d_ref[0] * rows, rows), rows), :].astype(bf16)
 
 
-def gram_a_body(x_ref, g_ref, full_ref, gram_ref):
-    full_ref[: N_FSDP * MAIN] = x_ref[:, :, :CHUNK].reshape(N_FSDP * MAIN, CHUNK)
-    tail = x_ref[:, :, CHUNK:].reshape(N_FSDP * MAIN, 128)
+def gram_a_body(x0_ref, x1_ref, x2_ref, x3_ref, g_ref, full_ref, gram_ref):
+    tails = []
+    for k, x_ref in enumerate((x0_ref, x1_ref, x2_ref, x3_ref)):
+        full_ref[128 * k : 128 * k + 128] = x_ref[:, :, :CHUNK].reshape(128, CHUNK)
+        tails.append(x_ref[:, :, CHUNK:].reshape(128, 128))
+    tail = jnp.concatenate(tails, axis=0)
     rows = 2 * N_FSDP
     r = lax.broadcasted_iota(jnp.int32, (rows, N_FSDP * MAIN), 0)
     c = lax.broadcasted_iota(jnp.int32, (rows, N_FSDP * MAIN), 1)
@@ -276,7 +291,7 @@
 def local(kva_parts, kvb_parts, kva_moment, kvb_moment):
     y = lax.axis_index("y").astype(jnp.int32).reshape(1)
     c = lax.axis_index("c").astype(jnp.int32).reshape(1)
-    f = lax.axis_index(FSDP).astype(jnp.int32).reshape(1)
+    z = lax.axis_index("z").astype(jnp.int32).reshape(1)
     d = y * 2 + c
     rows_b = KV_RANK // N_DP
 
@@ -296,46 +311,51 @@
     grads_b = others(grad_b, "y", 4)
     grad_a, push_a = call(
         push_a_body,
-        (shape((MAIN, WIDE), bf16), shape((N_FSDP, MAIN, WIDE), bf16)),
+        (shape((2 * MAIN, KV_RANK), bf16), shape((8, MAIN, WIDE), bf16)),
         1,
         2,
     )(d, terms_a, kva_moment)
-    all_a = exchange(push_a, FSDP)
-
-    grad_b = lax.all_gather(pair_sums(grads_b), "c", tiled=True)
-    moment_b, long_b, piece_b = call(
+    all_z = exchange(push_a, "z")
+
+    rows = half.shape[0]
+    both = call(sum_b_body, shape((rows + 2 * MAIN, KV_RANK), bf16), 0, 5, flops=HINT)(
+        *grads_b, grad_a
+    )
+    both = lax.all_gather(both, "c")
+    all_z, both = lax.optimization_barrier((all_z, both))
+    all_a = others(all_z, "x", 4)
+    moment_b, long_b, piece_b, grad_a = call(
         moment_b_body,
         (
             shape(kvb_moment.shape, f32),
             shape(kvb_moment.shape, bf16),
             shape((rows_b, KV_RANK), bf16),
+            shape((2, 2 * MAIN, KV_RANK), bf16),
         ),
         1,
         2,
         [pltpu.VMEM((KV_RANK, KV_RANK), f32)],
-        flops=HINT,
-    )(d, grad_b, kvb_moment)
-    piece_b, grad_a = lax.optimization_barrier((piece_b, grad_a))
-    terms_b = others(sum_over(piece_b, "x", 4), "z", 8, 2)
-
-    grads_a = others(lax.all_gather(grad_a, "c"), "y", 4)
+    )(d, both, kvb_moment)
+    terms_b = others(sum_pair(piece_b, "z", 8), "z", 8, 2)
+
+    grads_a = others(grad_a, "y", 4)
     moment_a = call(moment_a_body, shape(kva_moment.shape, f32), 1, 5)(y, *grads_a, kva_moment)
-    all_a, moment_a = lax.optimization_barrier((all_a, moment_a))
+    all_a[0], moment_a = lax.optimization_barrier((all_a[0], moment_a))
 
     gram_a, short_a = call(
         gram_a_body,
         (shape((2, 64 * BLOCKS, 384), bf16), shape((KVA_ROWS, CHUNK), bf16)),
         0,
-        1,
+        4,
         [pltpu.VMEM((128 * BLOCKS, 128 * BLOCKS), f32)],
-    )(all_a)
+    )(*all_a)
     gram_a = lax.all_gather(gram_a, "c")
     gram_a = lax.dynamic_index_in_dim(gram_a, lax.axis_index("c"), axis=1, keepdims=False)
     gram_a = total_of(gram_a).astype(bf16)
     _, terms_b = lax.optimization_barrier((gram_a, terms_b))
     piece_b = pair_sums(terms_b)
     gram_a = lax.all_gather(sum_over(gram_a, "y", 4), "c")
-    piece_b = lax.all_gather(sum_pair(piece_b, "z", 8), "c", tiled=True)
+    piece_b = lax.all_gather(sum_over(piece_b, "x", 4), "c", tiled=True)
 
     pieces_b = others(piece_b, "y", 4)
     update_a = call(
@@ -345,7 +365,7 @@
         2,
         [pltpu.VMEM((128 * BLOCKS, 128 * BLOCKS), f32)]
         + [pltpu.VMEM((KVA_ROWS, KVA_ROWS), f32)] * 2,
-    )(f, gram_a, short_a)
+    )(z, gram_a, short_a)
     update_a, pieces_b = lax.optimization_barrier((update_a, pieces_b))
     update_a = call(unpack_body, shape(kva_moment.shape, bf16))(exchange(update_a, DP))
     update_b = call(

time: 108 us -> 107 us (level)
  starting transfers between devices: 53.5 us -> 49.1 us
  waiting for transfers between devices: 12.3 us -> 16.2 us
    all_to_all x3, starting transfers between devices: 17.9 us -> 14.8 us  [exchange(): return lax.all_to_all(x, axis, split_axis=0, concat_axis=0, tiled=True)]
    ppermute x1, starting transfers between devices: 3 us -> 0.25 us  [sum_pair(): other = lax.ppermute(x, axis, [(i, i ^ 1) for i in range(n)])]
    all_to_all x3, waiting for transfers between devices: 8.44 us -> 10.5 us  [exchange(): return lax.all_to_all(x, axis, split_axis=0, concat_axis=0, tiled=True)]
    ppermute x19 -> x22, waiting for transfers between devices: 3.86 us -> 5.67 us  [shift(): return lax.ppermute(x, axis, [(i, (i + k) % n) for i in range(n)])]
    all_gather x1, blocking collectives: 6.66 us -> 8.29 us  [local(): gram_a = lax.all_gather(sum_over(gram_a, 'y', 4), 'c')]
    all_gather x3 -> x2, blocking collectives: 9.93 us -> 8.49 us  [the longest x1 4.33 us: local(): piece_b = lax.all_gather(sum_over(piece_b, 'x', 4), 'c', tiled=True)]
    ppermute x19 -> x22, starting transfers between devices: 32.7 us -> 34 us  [shift(): return lax.ppermute(x, axis, [(i, (i + k) % n) for i in range(n)])]
  transfers between devices with their start and end apart: 23 -> 26, of which waited for: 3 -> 7; matrix products, arithmetic and copies ran while one was open for 0% -> 0% of each run, Pallas kernels for 15% -> 13%
where the time goes in v1:
time: 107 us
  starting transfers between devices  49.1 us (46%)
  blocking collectives  22.6 us (21%)
  Pallas kernels  18.1 us (17%)
  waiting for transfers between devices  16.2 us (15%)
    ppermute x22, starting transfers between devices, shift(): return lax.ppermute(x, axis, [(i, (i + k) % n) for i in range(n)])  34 us
    all_to_all x3, starting transfers between devices, exchange(): return lax.all_to_all(x, axis, split_axis=0, concat_axis=0, tiled=True)  14.8 us
    all_to_all x3, waiting for transfers between devices, exchange(): return lax.all_to_all(x, axis, split_axis=0, concat_axis=0, tiled=True)  10.5 us
    all_gather x1, blocking collectives, local(): gram_a = lax.all_gather(sum_over(gram_a, 'y', 4), 'c')  8.29 us
    pallas_call x1, Pallas kernels, local(): call(finish_a_body, shape((N_DP, MAIN, WIDE), bf16), 1, 2, [pltpu.VMEM((1...  6.64 us
    all_gather x1, blocking collectives, local(): gram_a = lax.all_gather(gram_a, 'c')  5.79 us
    ppermute x22, waiting for transfers between devices, shift(): return lax.ppermute(x, axis, [(i, (i + k) % n) for i in range(n)])  5.67 us
    pallas_call x1, Pallas kernels, local(): call(finish_b_body, shape(long_b.shape, bf16), 1, 5, [pltpu.VMEM((KV_RANK...  4.47 us
  transfers between devices with their start and end apart: 26, of which 7 were waited for; matrix products, arithmetic and copies ran while one was open for 0% of the time, Pallas kernels for 13%

profile of v1, /device:TPU:1, one launch (start us, length us, event | category | flops | bytes accessed | tf_op | source)
XLA Modules:
  0.0 107.0 jit_solution(846153719805314813)
XLA Ops:
  0.6 1.9 %shard_map.75 = (bf16[8,16,1024]{2,1,0:T(8,128)(2,1)}, bf16[256,512]{1,0:T(8,128)(2,1)}) custom-call(s32[1]{0:T(128)} %bitcast.1.c_ref, bf16[1,18,7168]{2,1,0:T(8,128)(2,1)} %a_ref.1, bf16[1,512,512]{2,1,0:T(8,128)(2,1)} %b_ref.3), custom_call_target="tpu_custom_call" | custom-call | tf_op jit(solution)/shard_map/pallas_call | solution.py:299
  2.5 3.3 %collective-permute-start = (bf16[256,512]{1,0:T(8,128)(2,1)}, bf16[256,512]{1,0:T(8,128)(2,1)S(1)}, u32[]{:S(2)}, u32[]{:S(2)}) collective-permute-start(bf16[256,512]{1,0:T(8,128)(2,1)} %get-tuple-element.30), channel_id=1, source_target_pairs={{0,32},{32,0},{1,33},{33,1},{2,34},{34,2},{3,35},{35,3},{4,36},{36... | collective-permute-start | bytes 786440 | tf_op jit(solution)/shard_map/ppermute | solution.py:267
  5.8 3.5 %all-to-all-start = ((bf16[8,16,1024]{2,1,0:T(8,128)(2,1)}), bf16[8,16,1024]{2,1,0:T(8,128)(2,1)S(1)}, u32[]{:S(2)}, u32[]{:S(2)}) async-start(bf16[8,16,1024]{2,1,0:T(8,128)(2,1)} %get-tuple-element.29), calls=%async_computation | async-start | bytes 524288 | tf_op jit(solution)/shard_map/all_to_all | solution.py:259
  9.4 0.1 shard_map.76.b0_ref
  9.4 6.4 %all-to-all-done.parts_ref = bf16[8,16,1024]{2,1,0:T(8,128)(2,1)S(1)} async-done(((bf16[8,16,1024]{2,1,0:T(8,128)(2,1)}), bf16[8,16,1024]{2,1,0:T(8,128)(2,1)S(1)}, u32[]{:S(2)}, u32[]{:S(2)}) %all-to-all-start) | async-done | bytes 262176 | tf_op jit(solution)/shard_map/all_to_all | solution.py:259
  15.8 0.3 collective-permute-start.1
  16.1 1.8 %collective-permute-start.2 = (bf16[256,512]{1,0:T(8,128)(2,1)S(1)}, bf16[256,512]{1,0:T(8,128)(2,1)S(1)}, u32[]{:S(2)}, u32[]{:S(2)}) collective-permute-start(bf16[256,512]{1,0:T(8,128)(2,1)S(1)} %shard_map.76.b0_ref), channel_id=1, source_target_pairs={{0,128},{64,192},{128,0},{192,64},{1,129},{65,193},{129,1},{193,65... | collective-permute-start | bytes 786440 | tf_op jit(solution)/shard_map/ppermute | solution.py:267
  17.9 0.6 collective-permute-start.3
  18.5 0.8 shard_map.77
  19.3 7.7 %all-to-all-start.1 = ((bf16[8,16,1024]{2,1,0:T(8,128)(2,1)}), bf16[8,16,1024]{2,1,0:T(8,128)(2,1)S(1)}, u32[]{:S(2)}, u32[]{:S(2)}) async-start(bf16[8,16,1024]{2,1,0:T(8,128)(2,1)} %get-tuple-element.32), calls=%async_computation.1 | async-start | bytes 524288 | tf_op jit(solution)/shard_map/all_to_all | solution.py:259
  27.0 1.9 %collective-permute-done.2.b2_ref = bf16[256,512]{1,0:T(8,128)(2,1)S(1)} collective-permute-done((bf16[256,512]{1,0:T(8,128)(2,1)S(1)}, bf16[256,512]{1,0:T(8,128)(2,1)S(1)}, u32[]{:S(2)}, u32[]{:S(2)}) %collective-permute-start.2) | collective-permute-done | bytes 262176 | tf_op jit(solution)/shard_map/ppermute | solution.py:267
  28.9 1.0 collective-permute-done.3.b3_ref
  29.8 0.1 shard_map.78
  30.0 4.2 %all-gather = bf16[576,512]{1,0:T(8,128)(2,1)S(1)} all-gather(bf16[288,512]{1,0:T(8,128)(2,1)S(1)} %shard_map.78), channel_id=2, replica_groups=mesh['y'=4,'c'=2,'x'=4,'z'=8] {'c'}, dimensions={0}, use_global_device_ids=true | all-gather | bytes 884736 | tf_op jit(solution)/shard_map/all_gather | solution.py:324
  34.1 2.1 %all-to-all-done.1.x0_ref = bf16[8,16,1024]{2,1,0:T(8,128)(2,1)S(1)} async-done(((bf16[8,16,1024]{2,1,0:T(8,128)(2,1)}), bf16[8,16,1024]{2,1,0:T(8,128)(2,1)S(1)}, u32[]{:S(2)}, u32[]{:S(2)}) %all-to-all-start.1) | async-done | bytes 262176 | tf_op jit(solution)/shard_map/all_to_all | solution.py:259
  36.2 1.2 %shard_map.79 = (f32[512,512]{1,0:T(8,128)}, bf16[512,512]{1,0:T(8,128)(2,1)S(1)}, bf16[64,512]{1,0:T(8,128)(2,1)S(1)}, bf16[2,32,512]{2,1,0:T(8,128)(2,1)S(1)}) custom-call(s32[1]{0:T(128)S(6)} %add.37.d_ref, bf16[2,288,512]{2,1,0:T(8,128)(2,1)S(1)} %bitcast.6, f32[512,512]{1,0:T(8,128)S(1)} %copy-done.2), custom_call_target="tpu_custom_call" | custom-call | tf_op jit(solution)/shard_map/pallas_call | solution.py:327
  37.4 1.0 collective-permute-start.4
  38.4 0.3 collective-permute-start.13
  38.6 1.2 %collective-permute-start.7 = (bf16[8,16,1024]{2,1,0:T(8,128)(2,1)S(1)}, bf16[8,16,1024]{2,1,0:T(8,128)(2,1)S(1)}, u32[]{:S(2)}, u32[]{:S(2)}) collective-permute-start(bf16[8,16,1024]{2,1,0:T(8,128)(2,1)S(1)} %all-to-all-done.1.x0_ref), channel_id=1, source_target_pairs={{0,8},{8,16},{16,24},{24,0},{1,9},{9,17},{17,25},{25,1},{2,10},{10... | collective-permute-start | bytes 786440 | tf_op jit(solution)/shard_map/ppermute | solution.py:267
  39.8 2.5 %collective-permute-start.8 = (bf16[8,16,1024]{2,1,0:T(8,128)(2,1)S(1)}, bf16[8,16,1024]{2,1,0:T(8,128)(2,1)S(1)}, u32[]{:S(2)}, u32[]{:S(2)}) collective-permute-start(bf16[8,16,1024]{2,1,0:T(8,128)(2,1)S(1)} %all-to-all-done.1.x0_ref), channel_id=1, source_target_pairs={{0,16},{8,24},{16,0},{24,8},{1,17},{9,25},{17,1},{25,9},{2,18},{10... | collective-permute-start | bytes 786440 | tf_op jit(solution)/shard_map/ppermute | solution.py:267
  42.3 1.2 %collective-permute-start.9 = (bf16[8,16,1024]{2,1,0:T(8,128)(2,1)S(1)}, bf16[8,16,1024]{2,1,0:T(8,128)(2,1)S(1)}, u32[]{:S(2)}, u32[]{:S(2)}) collective-permute-start(bf16[8,16,1024]{2,1,0:T(8,128)(2,1)S(1)} %all-to-all-done.1.x0_ref), channel_id=1, source_target_pairs={{0,24},{8,0},{16,8},{24,16},{1,25},{9,1},{17,9},{25,17},{2,26},{10... | collective-permute-start | bytes 786440 | tf_op jit(solution)/shard_map/ppermute | solution.py:267
  43.5 1.5 %collective-permute-start.5 = (bf16[2,32,512]{2,1,0:T(8,128)(2,1)S(1)}, bf16[2,32,512]{2,1,0:T(8,128)(2,1)S(1)}, u32[]{:S(2)}, u32[]{:S(2)}) collective-permute-start(bf16[2,32,512]{2,1,0:T(8,128)(2,1)S(1)} %get-tuple-element.37.g0_ref), channel_id=1, source_target_pairs={{0,128},{64,192},{128,0},{192,64},{1,129},{65,193},{129,1},{193,65... | collective-permute-start | bytes 196616 | tf_op jit(solution)/shard_map/ppermute | solution.py:267
  45.0 2.1 %collective-permute-start.6 = (bf16[2,32,512]{2,1,0:T(8,128)(2,1)S(1)}, bf16[2,32,512]{2,1,0:T(8,128)(2,1)S(1)}, u32[]{:S(2)}, u32[]{:S(2)}) collective-permute-start(bf16[2,32,512]{2,1,0:T(8,128)(2,1)S(1)} %get-tuple-element.37.g0_ref), channel_id=1, source_target_pairs={{0,192},{64,0},{128,64},{192,128},{1,193},{65,1},{129,65},{193,129... | collective-permute-start | bytes 196616 | tf_op jit(solution)/shard_map/ppermute | solution.py:267
  47.0 1.0 collective-permute-done.5.g2_ref
  48.1 1.1 %collective-permute-start.14 = (bf16[64,512]{1,0:T(8,128)(2,1)S(1)}, bf16[64,512]{1,0:T(8,128)(2,1)S(1)}, u32[]{:S(2)}, u32[]{:S(2)}) collective-permute-start(bf16[64,512]{1,0:T(8,128)(2,1)S(1)} %add_convert_fusion.3), channel_id=1, source_target_pairs={{0,2},{1,3},{2,4},{3,5},{4,6},{5,7},{6,0},{7,1},{8,10},{9,11},{10,... | collective-permute-start | bytes 196616 | tf_op jit(solution)/shard_map/ppermute | solution.py:267
  49.2 4.8 %collective-permute-start.15 = (bf16[64,512]{1,0:T(8,128)(2,1)S(1)}, bf16[64,512]{1,0:T(8,128)(2,1)S(1)}, u32[]{:S(2)}, u32[]{:S(2)}) collective-permute-start(bf16[64,512]{1,0:T(8,128)(2,1)S(1)} %add_convert_fusion.3), channel_id=1, source_target_pairs={{0,4},{1,5},{2,6},{3,7},{4,0},{5,1},{6,2},{7,3},{8,12},{9,13},{10,... | collective-permute-start | bytes 196616 | tf_op jit(solution)/shard_map/ppermute | solution.py:267
  53.9 1.0 shard_map.80
  54.9 1.8 %collective-permute-start.16 = (bf16[64,512]{1,0:T(8,128)(2,1)S(1)}, bf16[64,512]{1,0:T(8,128)(2,1)S(1)}, u32[]{:S(2)}, u32[]{:S(2)}) collective-permute-start(bf16[64,512]{1,0:T(8,128)(2,1)S(1)} %add_convert_fusion.3), channel_id=1, source_target_pairs={{0,6},{1,7},{2,0},{3,1},{4,2},{5,3},{6,4},{7,5},{8,14},{9,15},{10,... | collective-permute-start | bytes 196616 | tf_op jit(solution)/shard_map/ppermute | solution.py:267
  56.7 1.3 %shard_map.81 = (bf16[2,320,384]{2,1,0:T(8,128)(2,1)S(1)}, bf16[576,896]{1,0:T(8,128)(2,1)S(1)}) custom-call(bf16[8,16,1024]{2,1,0:T(8,128)(2,1)S(1)} %all-to-all-done.1.x0_ref, bf16[8,16,1024]{2,1,0:T(8,128)(2,1)S(1)} %collective-permute-done.7.x1_ref, bf16[8,16,1024]{2,1,0:T(8,128)(2,1)S(1)} %collective-permute-done.8.x2_ref, ...), custom_call_target="tpu_custom_call" | custom-call | tf_op jit(solution)/shard_map/pallas_call | solution.py:345
  58.0 5.8 %all-gather.1 = bf16[4,320,384]{2,1,0:T(8,128)(2,1)S(1)} all-gather(bf16[2,320,384]{2,1,0:T(8,128)(2,1)S(1)} %get-tuple-element.41), channel_id=3, replica_groups=mesh['y'=4,'c'=2,'x'=4,'z'=8] {'c'}, dimensions={0}, use_global_device_ids=true | all-gather | bytes 1474560 | tf_op jit(solution)/shard_map/all_gather | solution.py:352
  63.8 0.1 dynamic-slice_reduce_fusion
  63.9 1.1 %collective-permute-start.19 = (bf16[64,512]{1,0:T(8,128)(2,1)S(1)}, bf16[64,512]{1,0:T(8,128)(2,1)S(1)}, u32[]{:S(2)}, u32[]{:S(2)}) collective-permute-start(bf16[64,512]{1,0:T(8,128)(2,1)S(1)} %add_convert_fusion.2), channel_id=1, source_target_pairs={{0,24},{8,0},{16,8},{24,16},{1,25},{9,1},{17,9},{25,17},{2,26},{10... | collective-permute-start | bytes 196616 | tf_op jit(solution)/shard_map/ppermute | solution.py:267
  65.1 0.6 collective-permute-start.18
  65.7 1.1 %collective-permute-start.17 = (bf16[64,512]{1,0:T(8,128)(2,1)S(1)}, bf16[64,512]{1,0:T(8,128)(2,1)S(1)}, u32[]{:S(2)}, u32[]{:S(2)}) collective-permute-start(bf16[64,512]{1,0:T(8,128)(2,1)S(1)} %add_convert_fusion.2), channel_id=1, source_target_pairs={{0,16},{8,24},{16,0},{24,8},{1,17},{9,25},{17,1},{25,9},{2,18},{10... | collective-permute-start | bytes 196616 | tf_op jit(solution)/shard_map/ppermute | solution.py:267
  66.8 2.0 %collective-permute-start.12 = (bf16[320,384]{1,0:T(8,128)(2,1)S(1)}, bf16[320,384]{1,0:T(8,128)(2,1)S(1)}, u32[]{:S(2)}, u32[]{:S(2)}) collective-permute-start(bf16[320,384]{1,0:T(8,128)(2,1)S(1)} %dynamic-slice_reduce_fusion), channel_id=1, source_target_pairs={{0,192},{64,0},{128,64},{192,128},{1,193},{65,1},{129,65},{193,129... | collective-permute-start | bytes 737288 | tf_op jit(solution)/shard_map/ppermute | solution.py:267
  68.8 2.0 %collective-permute-start.10 = (bf16[320,384]{1,0:T(8,128)(2,1)S(1)}, bf16[320,384]{1,0:T(8,128)(2,1)S(1)}, u32[]{:S(2)}, u32[]{:S(2)}) collective-permute-start(bf16[320,384]{1,0:T(8,128)(2,1)S(1)} %dynamic-slice_reduce_fusion), channel_id=1, source_target_pairs={{0,128},{64,192},{128,0},{192,64},{1,129},{65,193},{129,1},{193,65... | collective-permute-start | bytes 737288 | tf_op jit(solution)/shard_map/ppermute | solution.py:267
  70.9 4.3 %all_gather.27.g0_ref = bf16[128,512]{1,0:T(8,128)(2,1)S(1)} all-gather(bf16[64,512]{1,0:T(8,128)(2,1)S(1)} %add_convert_fusion.1), channel_id=1, replica_groups=mesh['y'=4,'c'=2,'x'=4,'z'=8] {'c'}, dimensions={0}, use_global_device_ids=true | all-gather | bytes 196608 | tf_op jit(solution)/shard_map/all_gather | solution.py:358
  75.3 1.6 %collective-permute-start.20 = (bf16[128,512]{1,0:T(8,128)(2,1)S(1)}, bf16[128,512]{1,0:T(8,128)(2,1)S(1)}, u32[]{:S(2)}, u32[]{:S(2)}) collective-permute-start(bf16[128,512]{1,0:T(8,128)(2,1)S(1)} %all_gather.27.g0_ref), channel_id=1, source_target_pairs={{0,64},{64,128},{128,192},{192,0},{1,65},{65,129},{129,193},{193,1... | collective-permute-start | bytes 393224 | tf_op jit(solution)/shard_map/ppermute | solution.py:267
  76.8 1.7 %collective-permute-start.21 = (bf16[128,512]{1,0:T(8,128)(2,1)S(1)}, bf16[128,512]{1,0:T(8,128)(2,1)S(1)}, u32[]{:S(2)}, u32[]{:S(2)}) collective-permute-start(bf16[128,512]{1,0:T(8,128)(2,1)S(1)} %all_gather.27.g0_ref), channel_id=1, source_target_pairs={{0,128},{64,192},{128,0},{192,64},{1,129},{65,193},{129,1},{193,65... | collective-permute-start | bytes 393224 | tf_op jit(solution)/shard_map/ppermute | solution.py:267
  78.6 0.7 collective-permute-start.22
  79.2 1.7 %collective-permute-done.10 = bf16[320,384]{1,0:T(8,128)(2,1)S(1)} collective-permute-done((bf16[320,384]{1,0:T(8,128)(2,1)S(1)}, bf16[320,384]{1,0:T(8,128)(2,1)S(1)}, u32[]{:S(2)}, u32[]{:S(2)}) %collective-permute-start.10) | collective-permute-done | bytes 245792 | tf_op jit(solution)/shard_map/ppermute | solution.py:267
  80.9 0.1 add_convert_fusion
  81.1 8.3 %all-gather.2 = bf16[640,384]{1,0:T(8,128)(2,1)S(1)} all-gather(bf16[320,384]{1,0:T(8,128)(2,1)S(1)} %add_convert_fusion), channel_id=4, replica_groups=mesh['y'=4,'c'=2,'x'=4,'z'=8] {'c'}, dimensions={0}, use_global_device_ids=true | all-gather | bytes 737280 | tf_op jit(solution)/shard_map/all_gather | solution.py:357
  89.4 6.6 %shard_map.82 = bf16[8,16,1024]{2,1,0:T(8,128)(2,1)} custom-call(s32[1]{0:T(128)} %bitcast.3.f_ref, bf16[2,320,384]{2,1,0:T(8,128)(2,1)S(1)} %bitcast.7, bf16[576,896]{1,0:T(8,128)(2,1)S(1)} %get-tuple-element.42.x_ref), custom_call_target="tpu_custom_call" | custom-call | tf_op jit(solution)/shard_map/pallas_call | solution.py:361
  96.0 3.7 %all-to-all-start.2 = ((bf16[8,16,1024]{2,1,0:T(8,128)(2,1)}), bf16[8,16,1024]{2,1,0:T(8,128)(2,1)S(1)}, u32[]{:S(2)}, u32[]{:S(2)}) async-start(bf16[8,16,1024]{2,1,0:T(8,128)(2,1)} %shard_map.82), calls=%async_computation.2 | async-start | bytes 524288 | tf_op jit(solution)/shard_map/all_to_all | solution.py:259
  99.7 4.5 %shard_map.84 = bf16[512,512]{1,0:T(8,128)(2,1)} custom-call(s32[1]{0:T(128)} %bitcast.i_ref, bf16[128,512]{1,0:T(8,128)(2,1)S(1)} %all_gather.27.g0_ref, bf16[128,512]{1,0:T(8,128)(2,1)S(1)} %collective-permute-done.20.g1_ref, bf16[128,512]{1,0:T(8,128)(2,1)S(1)} %collective-permute-done.21.g2_ref, bf16[128,512]{1,0:T(8,128)(2,1)S(1)} %collective-permute-done.22.g3_ref, ...), custom_call_target="tpu_custom_call" | custom-call | tf_op jit(solution)/shard_map/pallas_call | solution.py:371
  104.2 2.0 %all-to-all-done.2.u_ref = bf16[8,16,1024]{2,1,0:T(8,128)(2,1)S(1)} async-done(((bf16[8,16,1024]{2,1,0:T(8,128)(2,1)}), bf16[8,16,1024]{2,1,0:T(8,128)(2,1)S(1)}, u32[]{:S(2)}, u32[]{:S(2)}) %all-to-all-start.2) | async-done | bytes 262176 | tf_op jit(solution)/shard_map/all_to_all | solution.py:259
  106.2 0.8 shard_map.83
  (29 shorter events, 0.2 us)
Async XLA Ops:
  2.5 6.9 %copy-start.1 = (bf16[1,512,512]{2,1,0:T(8,128)(2,1)S(1)}, bf16[1,512,512]{2,1,0:T(8,128)(2,1)}, u32[]{:S(2)}) copy-start(bf16[1,512,512]{2,1,0:T(8,128)(2,1)} %b_ref.3) | copy-start | bytes 1572868
  2.5 6.8 %collective-permute-start = (bf16[256,512]{1,0:T(8,128)(2,1)}, bf16[256,512]{1,0:T(8,128)(2,1)S(1)}, u32[]{:S(2)}, u32[]{:S(2)}) collective-permute-start(bf16[256,512]{1,0:T(8,128)(2,1)} %get-tuple-element.30), channel_id=1, source_target_pairs={{0,32},{32,0},{1,33},{33,1},{2,34},{34,2},{3,35},{35,3},{4,36},{36... | collective-permute-start | bytes 786440 | tf_op jit(solution)/shard_map/ppermute | solution.py:267
  5.8 12.7 %copy-start = (f32[18,7168]{1,0:T(8,128)S(1)}, f32[18,7168]{1,0:T(8,128)}, u32[]{:S(2)}) copy-start(f32[18,7168]{1,0:T(8,128)} %m_ref.5) | copy-start | bytes 1548292
  5.8 10.0 %all-to-all-start = ((bf16[8,16,1024]{2,1,0:T(8,128)(2,1)}), bf16[8,16,1024]{2,1,0:T(8,128)(2,1)S(1)}, u32[]{:S(2)}, u32[]{:S(2)}) async-start(bf16[8,16,1024]{2,1,0:T(8,128)(2,1)} %get-tuple-element.29), calls=%async_computation | async-start | bytes 524288 | tf_op jit(solution)/shard_map/all_to_all | solution.py:259
  15.8 11.1 %collective-permute-start.1 = (bf16[256,512]{1,0:T(8,128)(2,1)S(1)}, bf16[256,512]{1,0:T(8,128)(2,1)S(1)}, u32[]{:S(2)}, u32[]{:S(2)}) collective-permute-start(bf16[256,512]{1,0:T(8,128)(2,1)S(1)} %shard_map.76.b0_ref), channel_id=1, source_target_pairs={{0,64},{64,128},{128,192},{192,0},{1,65},{65,129},{129,193},{193,1... | collective-permute-start | bytes 786440 | tf_op jit(solution)/shard_map/ppermute | solution.py:267
  16.1 12.7 %collective-permute-start.2 = (bf16[256,512]{1,0:T(8,128)(2,1)S(1)}, bf16[256,512]{1,0:T(8,128)(2,1)S(1)}, u32[]{:S(2)}, u32[]{:S(2)}) collective-permute-start(bf16[256,512]{1,0:T(8,128)(2,1)S(1)} %shard_map.76.b0_ref), channel_id=1, source_target_pairs={{0,128},{64,192},{128,0},{192,64},{1,129},{65,193},{129,1},{193,65... | collective-permute-start | bytes 786440 | tf_op jit(solution)/shard_map/ppermute | solution.py:267
  17.9 11.9 %collective-permute-start.3 = (bf16[256,512]{1,0:T(8,128)(2,1)S(1)}, bf16[256,512]{1,0:T(8,128)(2,1)S(1)}, u32[]{:S(2)}, u32[]{:S(2)}) collective-permute-start(bf16[256,512]{1,0:T(8,128)(2,1)S(1)} %shard_map.76.b0_ref), channel_id=1, source_target_pairs={{0,192},{64,0},{128,64},{192,128},{1,193},{65,1},{129,65},{193,129... | collective-permute-start | bytes 786440 | tf_op jit(solution)/shard_map/ppermute | solution.py:267
  19.3 16.9 %all-to-all-start.1 = ((bf16[8,16,1024]{2,1,0:T(8,128)(2,1)}), bf16[8,16,1024]{2,1,0:T(8,128)(2,1)S(1)}, u32[]{:S(2)}, u32[]{:S(2)}) async-start(bf16[8,16,1024]{2,1,0:T(8,128)(2,1)} %get-tuple-element.32), calls=%async_computation.1 | async-start | bytes 524288 | tf_op jit(solution)/shard_map/all_to_all | solution.py:259
  29.8 6.4 %copy-start.2 = (f32[512,512]{1,0:T(8,128)S(1)}, f32[512,512]{1,0:T(8,128)}, u32[]{:S(2)}) copy-start(f32[512,512]{1,0:T(8,128)} %m_ref.4) | copy-start | bytes 3145732
  37.4 6.0 %collective-permute-start.4 = (bf16[2,32,512]{2,1,0:T(8,128)(2,1)S(1)}, bf16[2,32,512]{2,1,0:T(8,128)(2,1)S(1)}, u32[]{:S(2)}, u32[]{:S(2)}) collective-permute-start(bf16[2,32,512]{2,1,0:T(8,128)(2,1)S(1)} %get-tuple-element.37.g0_ref), channel_id=1, source_target_pairs={{0,64},{64,128},{128,192},{192,0},{1,65},{65,129},{129,193},{193,1... | collective-permute-start | bytes 196616 | tf_op jit(solution)/shard_map/ppermute | solution.py:267
  38.4 6.6 %collective-permute-start.13 = (bf16[64,512]{1,0:T(8,128)(2,1)S(1)}, bf16[64,512]{1,0:T(8,128)(2,1)S(1)}, u32[]{:S(2)}, u32[]{:S(2)}) collective-permute-start(bf16[64,512]{1,0:T(8,128)(2,1)S(1)} %get-tuple-element.43), channel_id=1, source_target_pairs={{0,1},{1,0},{2,3},{3,2},{4,5},{5,4},{6,7},{7,6},{8,9},{9,8},{10,11... | collective-permute-start | bytes 196616 | tf_op jit(solution)/shard_map/ppermute | solution.py:287
  38.6 16.3 %collective-permute-start.7 = (bf16[8,16,1024]{2,1,0:T(8,128)(2,1)S(1)}, bf16[8,16,1024]{2,1,0:T(8,128)(2,1)S(1)}, u32[]{:S(2)}, u32[]{:S(2)}) collective-permute-start(bf16[8,16,1024]{2,1,0:T(8,128)(2,1)S(1)} %all-to-all-done.1.x0_ref), channel_id=1, source_target_pairs={{0,8},{8,16},{16,24},{24,0},{1,9},{9,17},{17,25},{25,1},{2,10},{10... | collective-permute-start | bytes 786440 | tf_op jit(solution)/shard_map/ppermute | solution.py:267
  39.8 16.9 %collective-permute-start.8 = (bf16[8,16,1024]{2,1,0:T(8,128)(2,1)S(1)}, bf16[8,16,1024]{2,1,0:T(8,128)(2,1)S(1)}, u32[]{:S(2)}, u32[]{:S(2)}) collective-permute-start(bf16[8,16,1024]{2,1,0:T(8,128)(2,1)S(1)} %all-to-all-done.1.x0_ref), channel_id=1, source_target_pairs={{0,16},{8,24},{16,0},{24,8},{1,17},{9,25},{17,1},{25,9},{2,18},{10... | collective-permute-start | bytes 786440 | tf_op jit(solution)/shard_map/ppermute | solution.py:267
  42.3 14.4 %collective-permute-start.9 = (bf16[8,16,1024]{2,1,0:T(8,128)(2,1)S(1)}, bf16[8,16,1024]{2,1,0:T(8,128)(2,1)S(1)}, u32[]{:S(2)}, u32[]{:S(2)}) collective-permute-start(bf16[8,16,1024]{2,1,0:T(8,128)(2,1)S(1)} %all-to-all-done.1.x0_ref), channel_id=1, source_target_pairs={{0,24},{8,0},{16,8},{24,16},{1,25},{9,1},{17,9},{25,17},{2,26},{10... | collective-permute-start | bytes 786440 | tf_op jit(solution)/shard_map/ppermute | solution.py:267
  43.5 4.6 %collective-permute-start.5 = (bf16[2,32,512]{2,1,0:T(8,128)(2,1)S(1)}, bf16[2,32,512]{2,1,0:T(8,128)(2,1)S(1)}, u32[]{:S(2)}, u32[]{:S(2)}) collective-permute-start(bf16[2,32,512]{2,1,0:T(8,128)(2,1)S(1)} %get-tuple-element.37.g0_ref), channel_id=1, source_target_pairs={{0,128},{64,192},{128,0},{192,64},{1,129},{65,193},{129,1},{193,65... | collective-permute-start | bytes 196616 | tf_op jit(solution)/shard_map/ppermute | solution.py:267
  45.0 4.2 %collective-permute-start.6 = (bf16[2,32,512]{2,1,0:T(8,128)(2,1)S(1)}, bf16[2,32,512]{2,1,0:T(8,128)(2,1)S(1)}, u32[]{:S(2)}, u32[]{:S(2)}) collective-permute-start(bf16[2,32,512]{2,1,0:T(8,128)(2,1)S(1)} %get-tuple-element.37.g0_ref), channel_id=1, source_target_pairs={{0,192},{64,0},{128,64},{192,128},{1,193},{65,1},{129,65},{193,129... | collective-permute-start | bytes 196616 | tf_op jit(solution)/shard_map/ppermute | solution.py:267
  48.1 15.8 %collective-permute-start.14 = (bf16[64,512]{1,0:T(8,128)(2,1)S(1)}, bf16[64,512]{1,0:T(8,128)(2,1)S(1)}, u32[]{:S(2)}, u32[]{:S(2)}) collective-permute-start(bf16[64,512]{1,0:T(8,128)(2,1)S(1)} %add_convert_fusion.3), channel_id=1, source_target_pairs={{0,2},{1,3},{2,4},{3,5},{4,6},{5,7},{6,0},{7,1},{8,10},{9,11},{10,... | collective-permute-start | bytes 196616 | tf_op jit(solution)/shard_map/ppermute | solution.py:267
  49.2 14.7 %collective-permute-start.15 = (bf16[64,512]{1,0:T(8,128)(2,1)S(1)}, bf16[64,512]{1,0:T(8,128)(2,1)S(1)}, u32[]{:S(2)}, u32[]{:S(2)}) collective-permute-start(bf16[64,512]{1,0:T(8,128)(2,1)S(1)} %add_convert_fusion.3), channel_id=1, source_target_pairs={{0,4},{1,5},{2,6},{3,7},{4,0},{5,1},{6,2},{7,3},{8,12},{9,13},{10,... | collective-permute-start | bytes 196616 | tf_op jit(solution)/shard_map/ppermute | solution.py:267
  54.9 9.0 %collective-permute-start.16 = (bf16[64,512]{1,0:T(8,128)(2,1)S(1)}, bf16[64,512]{1,0:T(8,128)(2,1)S(1)}, u32[]{:S(2)}, u32[]{:S(2)}) collective-permute-start(bf16[64,512]{1,0:T(8,128)(2,1)S(1)} %add_convert_fusion.3), channel_id=1, source_target_pairs={{0,6},{1,7},{2,0},{3,1},{4,2},{5,3},{6,4},{7,5},{8,14},{9,15},{10,... | collective-permute-start | bytes 196616 | tf_op jit(solution)/shard_map/ppermute | solution.py:267
  63.9 4.9 %collective-permute-start.19 = (bf16[64,512]{1,0:T(8,128)(2,1)S(1)}, bf16[64,512]{1,0:T(8,128)(2,1)S(1)}, u32[]{:S(2)}, u32[]{:S(2)}) collective-permute-start(bf16[64,512]{1,0:T(8,128)(2,1)S(1)} %add_convert_fusion.2), channel_id=1, source_target_pairs={{0,24},{8,0},{16,8},{24,16},{1,25},{9,1},{17,9},{25,17},{2,26},{10... | collective-permute-start | bytes 196616 | tf_op jit(solution)/shard_map/ppermute | solution.py:267
  65.1 5.8 %collective-permute-start.18 = (bf16[64,512]{1,0:T(8,128)(2,1)S(1)}, bf16[64,512]{1,0:T(8,128)(2,1)S(1)}, u32[]{:S(2)}, u32[]{:S(2)}) collective-permute-start(bf16[64,512]{1,0:T(8,128)(2,1)S(1)} %add_convert_fusion.2), channel_id=1, source_target_pairs={{0,8},{8,16},{16,24},{24,0},{1,9},{9,17},{17,25},{25,1},{2,10},{10... | collective-permute-start | bytes 196616 | tf_op jit(solution)/shard_map/ppermute | solution.py:267
  65.7 5.2 %collective-permute-start.17 = (bf16[64,512]{1,0:T(8,128)(2,1)S(1)}, bf16[64,512]{1,0:T(8,128)(2,1)S(1)}, u32[]{:S(2)}, u32[]{:S(2)}) collective-permute-start(bf16[64,512]{1,0:T(8,128)(2,1)S(1)} %add_convert_fusion.2), channel_id=1, source_target_pairs={{0,16},{8,24},{16,0},{24,8},{1,17},{9,25},{17,1},{25,9},{2,18},{10... | collective-permute-start | bytes 196616 | tf_op jit(solution)/shard_map/ppermute | solution.py:267
  66.8 11.8 %collective-permute-start.12 = (bf16[320,384]{1,0:T(8,128)(2,1)S(1)}, bf16[320,384]{1,0:T(8,128)(2,1)S(1)}, u32[]{:S(2)}, u32[]{:S(2)}) collective-permute-start(bf16[320,384]{1,0:T(8,128)(2,1)S(1)} %dynamic-slice_reduce_fusion), channel_id=1, source_target_pairs={{0,192},{64,0},{128,64},{192,128},{1,193},{65,1},{129,65},{193,129... | collective-permute-start | bytes 737288 | tf_op jit(solution)/shard_map/ppermute | solution.py:267
  68.8 10.4 %collective-permute-start.11 = (bf16[320,384]{1,0:T(8,128)(2,1)S(1)}, bf16[320,384]{1,0:T(8,128)(2,1)S(1)}, u32[]{:S(2)}, u32[]{:S(2)}) collective-permute-start(bf16[320,384]{1,0:T(8,128)(2,1)S(1)} %dynamic-slice_reduce_fusion), channel_id=1, source_target_pairs={{0,64},{64,128},{128,192},{192,0},{1,65},{65,129},{129,193},{193,1... | collective-permute-start | bytes 737288 | tf_op jit(solution)/shard_map/ppermute | solution.py:267
  68.8 12.1 %collective-permute-start.10 = (bf16[320,384]{1,0:T(8,128)(2,1)S(1)}, bf16[320,384]{1,0:T(8,128)(2,1)S(1)}, u32[]{:S(2)}, u32[]{:S(2)}) collective-permute-start(bf16[320,384]{1,0:T(8,128)(2,1)S(1)} %dynamic-slice_reduce_fusion), channel_id=1, source_target_pairs={{0,128},{64,192},{128,0},{192,64},{1,129},{65,193},{129,1},{193,65... | collective-permute-start | bytes 737288 | tf_op jit(solution)/shard_map/ppermute | solution.py:267
  75.3 20.8 %collective-permute-start.20 = (bf16[128,512]{1,0:T(8,128)(2,1)S(1)}, bf16[128,512]{1,0:T(8,128)(2,1)S(1)}, u32[]{:S(2)}, u32[]{:S(2)}) collective-permute-start(bf16[128,512]{1,0:T(8,128)(2,1)S(1)} %all_gather.27.g0_ref), channel_id=1, source_target_pairs={{0,64},{64,128},{128,192},{192,0},{1,65},{65,129},{129,193},{193,1... | collective-permute-start | bytes 393224 | tf_op jit(solution)/shard_map/ppermute | solution.py:267
  76.8 19.2 %collective-permute-start.21 = (bf16[128,512]{1,0:T(8,128)(2,1)S(1)}, bf16[128,512]{1,0:T(8,128)(2,1)S(1)}, u32[]{:S(2)}, u32[]{:S(2)}) collective-permute-start(bf16[128,512]{1,0:T(8,128)(2,1)S(1)} %all_gather.27.g0_ref), channel_id=1, source_target_pairs={{0,128},{64,192},{128,0},{192,64},{1,129},{65,193},{129,1},{193,65... | collective-permute-start | bytes 393224 | tf_op jit(solution)/shard_map/ppermute | solution.py:267
  78.6 17.5 %collective-permute-start.22 = (bf16[128,512]{1,0:T(8,128)(2,1)S(1)}, bf16[128,512]{1,0:T(8,128)(2,1)S(1)}, u32[]{:S(2)}, u32[]{:S(2)}) collective-permute-start(bf16[128,512]{1,0:T(8,128)(2,1)S(1)} %all_gather.27.g0_ref), channel_id=1, source_target_pairs={{0,192},{64,0},{128,64},{192,128},{1,193},{65,1},{129,65},{193,129... | collective-permute-start | bytes 393224 | tf_op jit(solution)/shard_map/ppermute | solution.py:267
  96.0 10.2 %all-to-all-start.2 = ((bf16[8,16,1024]{2,1,0:T(8,128)(2,1)}), bf16[8,16,1024]{2,1,0:T(8,128)(2,1)S(1)}, u32[]{:S(2)}, u32[]{:S(2)}) async-start(bf16[8,16,1024]{2,1,0:T(8,128)(2,1)} %shard_map.82), calls=%async_computation.2 | async-start | bytes 524288 | tf_op jit(solution)/shard_map/all_to_all | solution.py:259

commit v2 on v1

--- a/solution.py
+++ b/solution.py
@@ -92,7 +92,10 @@
         for c in range(2):
             start = (((i_ref[0] - k) & 3) * 2 + c) * CHUNK
             lanes = pl.ds(pl.multiple_of(start, 128), CHUNK)
-            grad = jnp.concatenate([g_ref[c, :MAIN], g_ref[c, MAIN:]], axis=1).astype(f32)
+            first = KV_RANK // 4 + 2 * MAIN * c
+            low = g_ref[first : first + MAIN]
+            high = g_ref[first + MAIN : first + 2 * MAIN]
+            grad = jnp.concatenate([low, high], axis=1).astype(f32)
             main = grad[:, :CHUNK]
             o_ref[:MAIN, lanes] = decay_rate * m_ref[:MAIN, lanes] + main
             tail = grad[:, CHUNK:]
@@ -128,7 +131,7 @@
     p_ref[...] = scratch[pl.ds(pl.multiple_of(d_ref[0] * rows, rows), rows), :].astype(bf16)
 
 
-def gram_a_body(x0_ref, x1_ref, x2_ref, x3_ref, g_ref, full_ref, gram_ref):
+def gram_a_body(c_ref, x0_ref, x1_ref, x2_ref, x3_ref, own_ref, send_ref, full_ref, gram_ref):
     tails = []
     for k, x_ref in enumerate((x0_ref, x1_ref, x2_ref, x3_ref)):
         full_ref[128 * k : 128 * k + 128] = x_ref[:, :, :CHUNK].reshape(128, CHUNK)
@@ -148,12 +151,12 @@
     gram_ref[:KVA_ROWS, :KVA_ROWS] = lax.dot_general(
         x, x, (((1,), (1,)), ((), ())), preferred_element_type=f32
     )
-    for i in range(BLOCKS):
-        for h in range(2):
-            rows = slice(128 * i + 64 * h, 128 * i + 64 * h + 64)
+    for h, o_ref in ((c_ref[0], own_ref), (1 - c_ref[0], send_ref)):
+        for i in range(BLOCKS):
+            rows = pl.ds(pl.multiple_of(128 * i + 64 * h, 64), 64)
             for j in range(3):
                 k = (i + j) % BLOCKS
-                g_ref[h, 64 * i : 64 * i + 64, 128 * j : 128 * j + 128] = gram_ref[
+                o_ref[64 * i : 64 * i + 64, 128 * j : 128 * j + 128] = gram_ref[
                     rows, 128 * k : 128 * k + 128
                 ].astype(bf16)
 
@@ -198,7 +201,7 @@
     rows = KV_RANK // 4
     for k, g_ref in enumerate((g0_ref, g1_ref, g2_ref, g3_ref)):
         first = pl.multiple_of(((i_ref[0] - k) & 3) * rows, rows)
-        gram_ref[pl.ds(first, rows), :] = g_ref[...].astype(f32)
+        gram_ref[pl.ds(first, rows), :] = g_ref[:rows].astype(f32)
     gram = gram_ref[...]
     s = gram_scale(gram)
     d01, g2 = two_steps(gram * (s * s))
@@ -338,26 +341,21 @@
     )(d, both, kvb_moment)
     terms_b = others(sum_pair(piece_b, "z", 8), "z", 8, 2)
 
-    grads_a = others(grad_a, "y", 4)
-    moment_a = call(moment_a_body, shape(kva_moment.shape, f32), 1, 5)(y, *grads_a, kva_moment)
-    all_a[0], moment_a = lax.optimization_barrier((all_a[0], moment_a))
-
-    gram_a, short_a = call(
+    part = shape((64 * BLOCKS, 384), bf16)
+    gram_a, send_a, short_a = call(
         gram_a_body,
-        (shape((2, 64 * BLOCKS, 384), bf16), shape((KVA_ROWS, CHUNK), bf16)),
-        0,
+        (part, part, shape((KVA_ROWS, CHUNK), bf16)),
+        1,
         4,
         [pltpu.VMEM((128 * BLOCKS, 128 * BLOCKS), f32)],
-    )(*all_a)
-    gram_a = lax.all_gather(gram_a, "c")
-    gram_a = lax.dynamic_index_in_dim(gram_a, lax.axis_index("c"), axis=1, keepdims=False)
-    gram_a = total_of(gram_a).astype(bf16)
-    _, terms_b = lax.optimization_barrier((gram_a, terms_b))
+    )(c, *all_a)
+    send_a, terms_b = lax.optimization_barrier((send_a, terms_b))
     piece_b = pair_sums(terms_b)
+    gram_a = pair_sums([gram_a, shift(send_a, "c", 2, 1)])
     gram_a = lax.all_gather(sum_over(gram_a, "y", 4), "c")
     piece_b = lax.all_gather(sum_over(piece_b, "x", 4), "c", tiled=True)
 
-    pieces_b = others(piece_b, "y", 4)
+    pieces_b = others(jnp.concatenate([piece_b, grad_a.reshape(-1, KV_RANK)]), "y", 4)
     update_a = call(
         finish_a_body,
         shape((N_DP, MAIN, WIDE), bf16),
@@ -367,6 +365,7 @@
         + [pltpu.VMEM((KVA_ROWS, KVA_ROWS), f32)] * 2,
     )(z, gram_a, short_a)
     update_a, pieces_b = lax.optimization_barrier((update_a, pieces_b))
+    moment_a = call(moment_a_body, shape(kva_moment.shape, f32), 1, 5)(y, *pieces_b, kva_moment)
     update_a = call(unpack_body, shape(kva_moment.shape, bf16))(exchange(update_a, DP))
     update_b = call(
         finish_b_body, shape(long_b.shape, bf16), 1, 5, [pltpu.VMEM((KV_RANK, KV_RANK), f32)]

time: 107 us -> 101 us (0.944)
  blocking collectives: 22.6 us -> 15 us
  starting transfers between devices: 49.1 us -> 50.3 us
    all_gather x1 -> x0, blocking collectives: 5.79 us -> none  [local(): gram_a = lax.all_gather(gram_a, 'c')]
    ppermute x22 -> x20, starting transfers between devices: 34 us -> 35.3 us  [shift(): return lax.ppermute(x, axis, [(i, (i + k) % n) for i in range(n)])]
    all_gather x1, blocking collectives: 4.33 us -> 3.05 us  [local(): piece_b = lax.all_gather(sum_over(piece_b, 'x', 4), 'c', tiled=True)]
    ppermute x22 -> x20, waiting for transfers between devices: 5.67 us -> 6.34 us  [shift(): return lax.ppermute(x, axis, [(i, (i + k) % n) for i in range(n)])]
  transfers between devices with their start and end apart: 26 -> 24, of which waited for: 7 -> 7; matrix products, arithmetic and copies ran while one was open for 0% -> 0% of each run, Pallas kernels for 13% -> 14%
where the time goes in v2:
time: 101 us; the launch traced here: 100 us
  starting transfers between devices  50.3 us (50%)
  Pallas kernels  18.2 us (18%)
  waiting for transfers between devices  15.9 us (16%)
  blocking collectives  15 us (15%)
    ppermute x20, starting transfers between devices, shift(): return lax.ppermute(x, axis, [(i, (i + k) % n) for i in range(n)])  35.3 us
    all_to_all x3, starting transfers between devices, exchange(): return lax.all_to_all(x, axis, split_axis=0, concat_axis=0, tiled=True)  14.8 us
    all_to_all x3, waiting for transfers between devices, exchange(): return lax.all_to_all(x, axis, split_axis=0, concat_axis=0, tiled=True)  9.56 us
    all_gather x1, blocking collectives, local(): gram_a = lax.all_gather(sum_over(gram_a, 'y', 4), 'c')  7.76 us
    pallas_call x1, Pallas kernels, local(): call(finish_a_body, shape((N_DP, MAIN, WIDE), bf16), 1, 2, [pltpu.VMEM((1...  6.64 us
    ppermute x20, waiting for transfers between devices, shift(): return lax.ppermute(x, axis, [(i, (i + k) % n) for i in range(n)])  6.34 us
    pallas_call x1, Pallas kernels, local(): call(finish_b_body, shape(long_b.shape, bf16), 1, 5, [pltpu.VMEM((KV_RANK...  4.47 us
    all_gather x1, blocking collectives, local(): both = lax.all_gather(both, 'c')  4.17 us
  transfers between devices with their start and end apart: 24, of which 7 were waited for; matrix products, arithmetic and copies ran while one was open for 0% of the time, Pallas kernels for 14%

profile of v2, /device:TPU:1, one launch (start us, length us, event | category | flops | bytes accessed | tf_op | source)
XLA Modules:
  0.0 100.4 jit_solution(10308971886287928325)
XLA Ops:
  0.6 1.9 %shard_map.75 = (bf16[8,16,1024]{2,1,0:T(8,128)(2,1)}, bf16[256,512]{1,0:T(8,128)(2,1)}) custom-call(s32[1]{0:T(128)} %bitcast.2.c_ref, bf16[1,18,7168]{2,1,0:T(8,128)(2,1)} %a_ref.1, bf16[1,512,512]{2,1,0:T(8,128)(2,1)} %b_ref.3), custom_call_target="tpu_custom_call" | custom-call | tf_op jit(solution)/shard_map/pallas_call | solution.py:302
  2.5 0.0 copy-start.1
  2.5 3.3 %collective-permute-start = (bf16[256,512]{1,0:T(8,128)(2,1)}, bf16[256,512]{1,0:T(8,128)(2,1)S(1)}, u32[]{:S(2)}, u32[]{:S(2)}) collective-permute-start(bf16[256,512]{1,0:T(8,128)(2,1)} %get-tuple-element.30), channel_id=1, source_target_pairs={{0,32},{32,0},{1,33},{33,1},{2,34},{34,2},{3,35},{35,3},{4,36},{36... | collective-permute-start | bytes 786440 | tf_op jit(solution)/shard_map/ppermute | solution.py:270
  5.8 3.5 %all-to-all-start = ((bf16[8,16,1024]{2,1,0:T(8,128)(2,1)}), bf16[8,16,1024]{2,1,0:T(8,128)(2,1)S(1)}, u32[]{:S(2)}, u32[]{:S(2)}) async-start(bf16[8,16,1024]{2,1,0:T(8,128)(2,1)} %get-tuple-element.29), calls=%async_computation | async-start | bytes 524288 | tf_op jit(solution)/shard_map/all_to_all | solution.py:262
  9.3 0.0 collective-permute-done.x_ref
  9.4 0.1 shard_map.76.b0_ref
  9.4 6.4 %all-to-all-done.parts_ref = bf16[8,16,1024]{2,1,0:T(8,128)(2,1)S(1)} async-done(((bf16[8,16,1024]{2,1,0:T(8,128)(2,1)}), bf16[8,16,1024]{2,1,0:T(8,128)(2,1)S(1)}, u32[]{:S(2)}, u32[]{:S(2)}) %all-to-all-start) | async-done | bytes 262176 | tf_op jit(solution)/shard_map/all_to_all | solution.py:262
  15.8 0.3 collective-permute-start.1
  16.1 1.8 %collective-permute-start.2 = (bf16[256,512]{1,0:T(8,128)(2,1)S(1)}, bf16[256,512]{1,0:T(8,128)(2,1)S(1)}, u32[]{:S(2)}, u32[]{:S(2)}) collective-permute-start(bf16[256,512]{1,0:T(8,128)(2,1)S(1)} %shard_map.76.b0_ref), channel_id=1, source_target_pairs={{0,128},{64,192},{128,0},{192,64},{1,129},{65,193},{129,1},{193,65... | collective-permute-start | bytes 786440 | tf_op jit(solution)/shard_map/ppermute | solution.py:270
  17.9 0.6 collective-permute-start.3
  18.5 0.8 shard_map.77
  19.3 7.7 %all-to-all-start.1 = ((bf16[8,16,1024]{2,1,0:T(8,128)(2,1)}), bf16[8,16,1024]{2,1,0:T(8,128)(2,1)S(1)}, u32[]{:S(2)}, u32[]{:S(2)}) async-start(bf16[8,16,1024]{2,1,0:T(8,128)(2,1)} %get-tuple-element.32), calls=%async_computation.1 | async-start | bytes 524288 | tf_op jit(solution)/shard_map/all_to_all | solution.py:262
  27.0 1.9 %collective-permute-done.2.b2_ref = bf16[256,512]{1,0:T(8,128)(2,1)S(1)} collective-permute-done((bf16[256,512]{1,0:T(8,128)(2,1)S(1)}, bf16[256,512]{1,0:T(8,128)(2,1)S(1)}, u32[]{:S(2)}, u32[]{:S(2)}) %collective-permute-start.2) | collective-permute-done | bytes 262176 | tf_op jit(solution)/shard_map/ppermute | solution.py:270
  28.9 1.0 collective-permute-done.3.b3_ref
  29.8 0.1 shard_map.78
  30.0 4.2 %all-gather = bf16[576,512]{1,0:T(8,128)(2,1)S(1)} all-gather(bf16[288,512]{1,0:T(8,128)(2,1)S(1)} %shard_map.78), channel_id=2, replica_groups=mesh['y'=4,'c'=2,'x'=4,'z'=8] {'c'}, dimensions={0}, use_global_device_ids=true | all-gather | bytes 884736 | tf_op jit(solution)/shard_map/all_gather | solution.py:327
  34.1 2.1 %all-to-all-done.1.x0_ref = bf16[8,16,1024]{2,1,0:T(8,128)(2,1)S(1)} async-done(((bf16[8,16,1024]{2,1,0:T(8,128)(2,1)}), bf16[8,16,1024]{2,1,0:T(8,128)(2,1)S(1)}, u32[]{:S(2)}, u32[]{:S(2)}) %all-to-all-start.1) | async-done | bytes 262176 | tf_op jit(solution)/shard_map/all_to_all | solution.py:262
  36.2 1.2 %shard_map.80 = (f32[512,512]{1,0:T(8,128)}, bf16[512,512]{1,0:T(8,128)(2,1)S(1)}, bf16[64,512]{1,0:T(8,128)(2,1)S(1)}, bf16[2,32,512]{2,1,0:T(8,128)(2,1)S(1)}) custom-call(s32[1]{0:T(128)S(6)} %add.36.d_ref, bf16[2,288,512]{2,1,0:T(8,128)(2,1)S(1)} %bitcast.6, f32[512,512]{1,0:T(8,128)S(1)} %copy-done.2), custom_call_target="tpu_custom_call" | custom-call | tf_op jit(solution)/shard_map/pallas_call | solution.py:330
  37.4 0.1 collective-permute-start.7
  37.5 1.2 %collective-permute-start.4 = (bf16[8,16,1024]{2,1,0:T(8,128)(2,1)S(1)}, bf16[8,16,1024]{2,1,0:T(8,128)(2,1)S(1)}, u32[]{:S(2)}, u32[]{:S(2)}) collective-permute-start(bf16[8,16,1024]{2,1,0:T(8,128)(2,1)S(1)} %all-to-all-done.1.x0_ref), channel_id=1, source_target_pairs={{0,8},{8,16},{16,24},{24,0},{1,9},{9,17},{17,25},{25,1},{2,10},{10... | collective-permute-start | bytes 786440 | tf_op jit(solution)/shard_map/ppermute | solution.py:270
  38.7 2.4 %collective-permute-start.5 = (bf16[8,16,1024]{2,1,0:T(8,128)(2,1)S(1)}, bf16[8,16,1024]{2,1,0:T(8,128)(2,1)S(1)}, u32[]{:S(2)}, u32[]{:S(2)}) collective-permute-start(bf16[8,16,1024]{2,1,0:T(8,128)(2,1)S(1)} %all-to-all-done.1.x0_ref), channel_id=1, source_target_pairs={{0,16},{8,24},{16,0},{24,8},{1,17},{9,25},{17,1},{25,9},{2,18},{10... | collective-permute-start | bytes 786440 | tf_op jit(solution)/shard_map/ppermute | solution.py:270
  41.2 1.2 %collective-permute-start.6 = (bf16[8,16,1024]{2,1,0:T(8,128)(2,1)S(1)}, bf16[8,16,1024]{2,1,0:T(8,128)(2,1)S(1)}, u32[]{:S(2)}, u32[]{:S(2)}) collective-permute-start(bf16[8,16,1024]{2,1,0:T(8,128)(2,1)S(1)} %all-to-all-done.1.x0_ref), channel_id=1, source_target_pairs={{0,24},{8,0},{16,8},{24,16},{1,25},{9,1},{17,9},{25,17},{2,26},{10... | collective-permute-start | bytes 786440 | tf_op jit(solution)/shard_map/ppermute | solution.py:270
  42.3 2.0 %collective-permute-start.8 = (bf16[64,512]{1,0:T(8,128)(2,1)S(1)}, bf16[64,512]{1,0:T(8,128)(2,1)S(1)}, u32[]{:S(2)}, u32[]{:S(2)}) collective-permute-start(bf16[64,512]{1,0:T(8,128)(2,1)S(1)} %add_convert_fusion.4), channel_id=1, source_target_pairs={{0,2},{1,3},{2,4},{3,5},{4,6},{5,7},{6,0},{7,1},{8,10},{9,11},{10,... | collective-permute-start | bytes 196616 | tf_op jit(solution)/shard_map/ppermute | solution.py:270
  44.4 4.2 %collective-permute-start.9 = (bf16[64,512]{1,0:T(8,128)(2,1)S(1)}, bf16[64,512]{1,0:T(8,128)(2,1)S(1)}, u32[]{:S(2)}, u32[]{:S(2)}) collective-permute-start(bf16[64,512]{1,0:T(8,128)(2,1)S(1)} %add_convert_fusion.4), channel_id=1, source_target_pairs={{0,4},{1,5},{2,6},{3,7},{4,0},{5,1},{6,2},{7,3},{8,12},{9,13},{10,... | collective-permute-start | bytes 196616 | tf_op jit(solution)/shard_map/ppermute | solution.py:270
  48.6 2.4 %collective-permute-start.10 = (bf16[64,512]{1,0:T(8,128)(2,1)S(1)}, bf16[64,512]{1,0:T(8,128)(2,1)S(1)}, u32[]{:S(2)}, u32[]{:S(2)}) collective-permute-start(bf16[64,512]{1,0:T(8,128)(2,1)S(1)} %add_convert_fusion.4), channel_id=1, source_target_pairs={{0,6},{1,7},{2,0},{3,1},{4,2},{5,3},{6,4},{7,5},{8,14},{9,15},{10,... | collective-permute-start | bytes 196616 | tf_op jit(solution)/shard_map/ppermute | solution.py:270
  51.0 1.4 %shard_map.79 = (bf16[320,384]{1,0:T(8,128)(2,1)S(1)}, bf16[320,384]{1,0:T(8,128)(2,1)S(1)}, bf16[576,896]{1,0:T(8,128)(2,1)S(1)}) custom-call(s32[1]{0:T(128)} %bitcast.2.c_ref, bf16[8,16,1024]{2,1,0:T(8,128)(2,1)S(1)} %all-to-all-done.1.x0_ref, bf16[8,16,1024]{2,1,0:T(8,128)(2,1)S(1)} %collective-permute-done.4.x1_ref, ...), custom_call_target="tpu_custom_call" | custom-call | tf_op jit(solution)/shard_map/pallas_call | solution.py:345
  52.4 1.2 %collective-permute-done.10 = bf16[64,512]{1,0:T(8,128)(2,1)S(1)} collective-permute-done((bf16[64,512]{1,0:T(8,128)(2,1)S(1)}, bf16[64,512]{1,0:T(8,128)(2,1)S(1)}, u32[]{:S(2)}, u32[]{:S(2)}) %collective-permute-start.10) | collective-permute-done | bytes 65568 | tf_op jit(solution)/shard_map/ppermute | solution.py:270
  53.6 4.9 %collective-permute-start.11 = (bf16[320,384]{1,0:T(8,128)(2,1)S(1)}, bf16[320,384]{1,0:T(8,128)(2,1)S(1)}, u32[]{:S(2)}, u32[]{:S(2)}) collective-permute-start(bf16[320,384]{1,0:T(8,128)(2,1)S(1)} %get-tuple-element.40), channel_id=1, source_target_pairs={{0,32},{32,0},{1,33},{33,1},{2,34},{34,2},{3,35},{35,3},{4,36},{36... | collective-permute-start | bytes 737288 | tf_op jit(solution)/shard_map/ppermute | solution.py:270
  58.5 0.4 collective-permute-start.17
  58.9 1.2 %collective-permute-start.16 = (bf16[64,512]{1,0:T(8,128)(2,1)S(1)}, bf16[64,512]{1,0:T(8,128)(2,1)S(1)}, u32[]{:S(2)}, u32[]{:S(2)}) collective-permute-start(bf16[64,512]{1,0:T(8,128)(2,1)S(1)} %add_convert_fusion.3), channel_id=1, source_target_pairs={{0,8},{8,16},{16,24},{24,0},{1,9},{9,17},{17,25},{25,1},{2,10},{10... | collective-permute-start | bytes 196616 | tf_op jit(solution)/shard_map/ppermute | solution.py:270
  60.1 0.6 collective-permute-start.15
  60.6 0.1 add_convert_fusion.1
  60.7 1.6 %collective-permute-start.14 = (bf16[320,384]{1,0:T(8,128)(2,1)S(1)}, bf16[320,384]{1,0:T(8,128)(2,1)S(1)}, u32[]{:S(2)}, u32[]{:S(2)}) collective-permute-start(bf16[320,384]{1,0:T(8,128)(2,1)S(1)} %add_convert_fusion.1), channel_id=1, source_target_pairs={{0,192},{64,0},{128,64},{192,128},{1,193},{65,1},{129,65},{193,129... | collective-permute-start | bytes 737288 | tf_op jit(solution)/shard_map/ppermute | solution.py:270
  62.3 0.0 collective-permute-done.17
  62.3 2.6 %collective-permute-start.12 = (bf16[320,384]{1,0:T(8,128)(2,1)S(1)}, bf16[320,384]{1,0:T(8,128)(2,1)S(1)}, u32[]{:S(2)}, u32[]{:S(2)}) collective-permute-start(bf16[320,384]{1,0:T(8,128)(2,1)S(1)} %add_convert_fusion.1), channel_id=1, source_target_pairs={{0,128},{64,192},{128,0},{192,64},{1,129},{65,193},{129,1},{193,65... | collective-permute-start | bytes 737288 | tf_op jit(solution)/shard_map/ppermute | solution.py:270
  64.9 3.1 %all_gather.19 = bf16[128,512]{1,0:T(8,128)(2,1)S(1)} all-gather(bf16[64,512]{1,0:T(8,128)(2,1)S(1)} %add_convert_fusion.2), channel_id=1, replica_groups=mesh['y'=4,'c'=2,'x'=4,'z'=8] {'c'}, dimensions={0}, use_global_device_ids=true | all-gather | bytes 196608 | tf_op jit(solution)/shard_map/all_gather | solution.py:356
  68.0 1.1 %collective-permute-start.18 = (bf16[192,512]{1,0:T(8,128)(2,1)S(1)}, bf16[192,512]{1,0:T(8,128)(2,1)S(1)}, u32[]{:S(2)}, u32[]{:S(2)}) collective-permute-start(bf16[192,512]{1,0:T(8,128)(2,1)S(1)} %pad_maximum_fusion.g0_ref), channel_id=1, source_target_pairs={{0,64},{64,128},{128,192},{192,0},{1,65},{65,129},{129,193},{193,1... | collective-permute-start | bytes 589832 | tf_op jit(solution)/shard_map/ppermute | solution.py:270
  69.1 1.6 %collective-permute-start.19 = (bf16[192,512]{1,0:T(8,128)(2,1)S(1)}, bf16[192,512]{1,0:T(8,128)(2,1)S(1)}, u32[]{:S(2)}, u32[]{:S(2)}) collective-permute-start(bf16[192,512]{1,0:T(8,128)(2,1)S(1)} %pad_maximum_fusion.g0_ref), channel_id=1, source_target_pairs={{0,128},{64,192},{128,0},{192,64},{1,129},{65,193},{129,1},{193,65... | collective-permute-start | bytes 589832 | tf_op jit(solution)/shard_map/ppermute | solution.py:270
  70.8 2.0 %collective-permute-start.20 = (bf16[192,512]{1,0:T(8,128)(2,1)S(1)}, bf16[192,512]{1,0:T(8,128)(2,1)S(1)}, u32[]{:S(2)}, u32[]{:S(2)}) collective-permute-start(bf16[192,512]{1,0:T(8,128)(2,1)S(1)} %pad_maximum_fusion.g0_ref), channel_id=1, source_target_pairs={{0,192},{64,0},{128,64},{192,128},{1,193},{65,1},{129,65},{193,129... | collective-permute-start | bytes 589832 | tf_op jit(solution)/shard_map/ppermute | solution.py:270
  72.7 2.2 %collective-permute-done.12 = bf16[320,384]{1,0:T(8,128)(2,1)S(1)} collective-permute-done((bf16[320,384]{1,0:T(8,128)(2,1)S(1)}, bf16[320,384]{1,0:T(8,128)(2,1)S(1)}, u32[]{:S(2)}, u32[]{:S(2)}) %collective-permute-start.12) | collective-permute-done | bytes 245792 | tf_op jit(solution)/shard_map/ppermute | solution.py:270
  74.9 0.1 add_convert_fusion
  75.0 7.8 %all-gather.1 = bf16[640,384]{1,0:T(8,128)(2,1)S(1)} all-gather(bf16[320,384]{1,0:T(8,128)(2,1)S(1)} %add_convert_fusion), channel_id=3, replica_groups=mesh['y'=4,'c'=2,'x'=4,'z'=8] {'c'}, dimensions={0}, use_global_device_ids=true | all-gather | bytes 737280 | tf_op jit(solution)/shard_map/all_gather | solution.py:355
  82.8 6.6 %shard_map.81 = bf16[8,16,1024]{2,1,0:T(8,128)(2,1)} custom-call(s32[1]{0:T(128)} %bitcast.1.f_ref, bf16[2,320,384]{2,1,0:T(8,128)(2,1)S(1)} %bitcast.7, bf16[576,896]{1,0:T(8,128)(2,1)S(1)} %get-tuple-element.41.x_ref), custom_call_target="tpu_custom_call" | custom-call | tf_op jit(solution)/shard_map/pallas_call | solution.py:359
  89.4 3.7 %all-to-all-start.2 = ((bf16[8,16,1024]{2,1,0:T(8,128)(2,1)}), bf16[8,16,1024]{2,1,0:T(8,128)(2,1)S(1)}, u32[]{:S(2)}, u32[]{:S(2)}) async-start(bf16[8,16,1024]{2,1,0:T(8,128)(2,1)} %shard_map.81), calls=%async_computation.2 | async-start | bytes 524288 | tf_op jit(solution)/shard_map/all_to_all | solution.py:262
  93.1 1.0 shard_map.82
  94.1 4.5 %shard_map.84 = bf16[512,512]{1,0:T(8,128)(2,1)} custom-call(s32[1]{0:T(128)} %bitcast.i_ref, bf16[192,512]{1,0:T(8,128)(2,1)S(1)} %pad_maximum_fusion.g0_ref, bf16[192,512]{1,0:T(8,128)(2,1)S(1)} %collective-permute-done.18.g1_ref, bf16[192,512]{1,0:T(8,128)(2,1)S(1)} %collective-permute-done.19.g2_ref, ...), custom_call_target="tpu_custom_call" | custom-call | tf_op jit(solution)/shard_map/pallas_call | solution.py:370
  98.6 1.1 %all-to-all-done.2.u_ref = bf16[8,16,1024]{2,1,0:T(8,128)(2,1)S(1)} async-done(((bf16[8,16,1024]{2,1,0:T(8,128)(2,1)}), bf16[8,16,1024]{2,1,0:T(8,128)(2,1)S(1)}, u32[]{:S(2)}, u32[]{:S(2)}) %all-to-all-start.2) | async-done | bytes 262176 | tf_op jit(solution)/shard_map/all_to_all | solution.py:262
  99.7 0.8 shard_map.83
  (25 shorter events, 0.2 us)
Async XLA Ops:
  2.5 6.9 %copy-start.1 = (bf16[1,512,512]{2,1,0:T(8,128)(2,1)S(1)}, bf16[1,512,512]{2,1,0:T(8,128)(2,1)}, u32[]{:S(2)}) copy-start(bf16[1,512,512]{2,1,0:T(8,128)(2,1)} %b_ref.3) | copy-start | bytes 1572868
  2.5 6.8 %collective-permute-start = (bf16[256,512]{1,0:T(8,128)(2,1)}, bf16[256,512]{1,0:T(8,128)(2,1)S(1)}, u32[]{:S(2)}, u32[]{:S(2)}) collective-permute-start(bf16[256,512]{1,0:T(8,128)(2,1)} %get-tuple-element.30), channel_id=1, source_target_pairs={{0,32},{32,0},{1,33},{33,1},{2,34},{34,2},{3,35},{35,3},{4,36},{36... | collective-permute-start | bytes 786440 | tf_op jit(solution)/shard_map/ppermute | solution.py:270
  5.8 12.7 %copy-start = (f32[18,7168]{1,0:T(8,128)S(1)}, f32[18,7168]{1,0:T(8,128)}, u32[]{:S(2)}) copy-start(f32[18,7168]{1,0:T(8,128)} %m_ref.5) | copy-start | bytes 1548292
  5.8 10.0 %all-to-all-start = ((bf16[8,16,1024]{2,1,0:T(8,128)(2,1)}), bf16[8,16,1024]{2,1,0:T(8,128)(2,1)S(1)}, u32[]{:S(2)}, u32[]{:S(2)}) async-start(bf16[8,16,1024]{2,1,0:T(8,128)(2,1)} %get-tuple-element.29), calls=%async_computation | async-start | bytes 524288 | tf_op jit(solution)/shard_map/all_to_all | solution.py:262
  15.8 11.1 %collective-permute-start.1 = (bf16[256,512]{1,0:T(8,128)(2,1)S(1)}, bf16[256,512]{1,0:T(8,128)(2,1)S(1)}, u32[]{:S(2)}, u32[]{:S(2)}) collective-permute-start(bf16[256,512]{1,0:T(8,128)(2,1)S(1)} %shard_map.76.b0_ref), channel_id=1, source_target_pairs={{0,64},{64,128},{128,192},{192,0},{1,65},{65,129},{129,193},{193,1... | collective-permute-start | bytes 786440 | tf_op jit(solution)/shard_map/ppermute | solution.py:270
  16.1 12.7 %collective-permute-start.2 = (bf16[256,512]{1,0:T(8,128)(2,1)S(1)}, bf16[256,512]{1,0:T(8,128)(2,1)S(1)}, u32[]{:S(2)}, u32[]{:S(2)}) collective-permute-start(bf16[256,512]{1,0:T(8,128)(2,1)S(1)} %shard_map.76.b0_ref), channel_id=1, source_target_pairs={{0,128},{64,192},{128,0},{192,64},{1,129},{65,193},{129,1},{193,65... | collective-permute-start | bytes 786440 | tf_op jit(solution)/shard_map/ppermute | solution.py:270
  17.9 11.9 %collective-permute-start.3 = (bf16[256,512]{1,0:T(8,128)(2,1)S(1)}, bf16[256,512]{1,0:T(8,128)(2,1)S(1)}, u32[]{:S(2)}, u32[]{:S(2)}) collective-permute-start(bf16[256,512]{1,0:T(8,128)(2,1)S(1)} %shard_map.76.b0_ref), channel_id=1, source_target_pairs={{0,192},{64,0},{128,64},{192,128},{1,193},{65,1},{129,65},{193,129... | collective-permute-start | bytes 786440 | tf_op jit(solution)/shard_map/ppermute | solution.py:270
  19.3 16.9 %all-to-all-start.1 = ((bf16[8,16,1024]{2,1,0:T(8,128)(2,1)}), bf16[8,16,1024]{2,1,0:T(8,128)(2,1)S(1)}, u32[]{:S(2)}, u32[]{:S(2)}) async-start(bf16[8,16,1024]{2,1,0:T(8,128)(2,1)} %get-tuple-element.32), calls=%async_computation.1 | async-start | bytes 524288 | tf_op jit(solution)/shard_map/all_to_all | solution.py:262
  29.8 6.4 %copy-start.2 = (f32[512,512]{1,0:T(8,128)S(1)}, f32[512,512]{1,0:T(8,128)}, u32[]{:S(2)}) copy-start(f32[512,512]{1,0:T(8,128)} %m_ref.4) | copy-start | bytes 3145732
  37.4 4.9 %collective-permute-start.7 = (bf16[64,512]{1,0:T(8,128)(2,1)S(1)}, bf16[64,512]{1,0:T(8,128)(2,1)S(1)}, u32[]{:S(2)}, u32[]{:S(2)}) collective-permute-start(bf16[64,512]{1,0:T(8,128)(2,1)S(1)} %get-tuple-element.39), channel_id=1, source_target_pairs={{0,1},{1,0},{2,3},{3,2},{4,5},{5,4},{6,7},{7,6},{8,9},{9,8},{10,11... | collective-permute-start | bytes 196616 | tf_op jit(solution)/shard_map/ppermute | solution.py:290
  37.5 11.1 %collective-permute-start.4 = (bf16[8,16,1024]{2,1,0:T(8,128)(2,1)S(1)}, bf16[8,16,1024]{2,1,0:T(8,128)(2,1)S(1)}, u32[]{:S(2)}, u32[]{:S(2)}) collective-permute-start(bf16[8,16,1024]{2,1,0:T(8,128)(2,1)S(1)} %all-to-all-done.1.x0_ref), channel_id=1, source_target_pairs={{0,8},{8,16},{16,24},{24,0},{1,9},{9,17},{17,25},{25,1},{2,10},{10... | collective-permute-start | bytes 786440 | tf_op jit(solution)/shard_map/ppermute | solution.py:270
  38.7 12.3 %collective-permute-start.5 = (bf16[8,16,1024]{2,1,0:T(8,128)(2,1)S(1)}, bf16[8,16,1024]{2,1,0:T(8,128)(2,1)S(1)}, u32[]{:S(2)}, u32[]{:S(2)}) collective-permute-start(bf16[8,16,1024]{2,1,0:T(8,128)(2,1)S(1)} %all-to-all-done.1.x0_ref), channel_id=1, source_target_pairs={{0,16},{8,24},{16,0},{24,8},{1,17},{9,25},{17,1},{25,9},{2,18},{10... | collective-permute-start | bytes 786440 | tf_op jit(solution)/shard_map/ppermute | solution.py:270
  41.2 9.8 %collective-permute-start.6 = (bf16[8,16,1024]{2,1,0:T(8,128)(2,1)S(1)}, bf16[8,16,1024]{2,1,0:T(8,128)(2,1)S(1)}, u32[]{:S(2)}, u32[]{:S(2)}) collective-permute-start(bf16[8,16,1024]{2,1,0:T(8,128)(2,1)S(1)} %all-to-all-done.1.x0_ref), channel_id=1, source_target_pairs={{0,24},{8,0},{16,8},{24,16},{1,25},{9,1},{17,9},{25,17},{2,26},{10... | collective-permute-start | bytes 786440 | tf_op jit(solution)/shard_map/ppermute | solution.py:270
  42.3 10.0 %collective-permute-start.8 = (bf16[64,512]{1,0:T(8,128)(2,1)S(1)}, bf16[64,512]{1,0:T(8,128)(2,1)S(1)}, u32[]{:S(2)}, u32[]{:S(2)}) collective-permute-start(bf16[64,512]{1,0:T(8,128)(2,1)S(1)} %add_convert_fusion.4), channel_id=1, source_target_pairs={{0,2},{1,3},{2,4},{3,5},{4,6},{5,7},{6,0},{7,1},{8,10},{9,11},{10,... | collective-permute-start | bytes 196616 | tf_op jit(solution)/shard_map/ppermute | solution.py:270
  44.4 8.0 %collective-permute-start.9 = (bf16[64,512]{1,0:T(8,128)(2,1)S(1)}, bf16[64,512]{1,0:T(8,128)(2,1)S(1)}, u32[]{:S(2)}, u32[]{:S(2)}) collective-permute-start(bf16[64,512]{1,0:T(8,128)(2,1)S(1)} %add_convert_fusion.4), channel_id=1, source_target_pairs={{0,4},{1,5},{2,6},{3,7},{4,0},{5,1},{6,2},{7,3},{8,12},{9,13},{10,... | collective-permute-start | bytes 196616 | tf_op jit(solution)/shard_map/ppermute | solution.py:270
  48.6 5.0 %collective-permute-start.10 = (bf16[64,512]{1,0:T(8,128)(2,1)S(1)}, bf16[64,512]{1,0:T(8,128)(2,1)S(1)}, u32[]{:S(2)}, u32[]{:S(2)}) collective-permute-start(bf16[64,512]{1,0:T(8,128)(2,1)S(1)} %add_convert_fusion.4), channel_id=1, source_target_pairs={{0,6},{1,7},{2,0},{3,1},{4,2},{5,3},{6,4},{7,5},{8,14},{9,15},{10,... | collective-permute-start | bytes 196616 | tf_op jit(solution)/shard_map/ppermute | solution.py:270
  53.6 7.0 %collective-permute-start.11 = (bf16[320,384]{1,0:T(8,128)(2,1)S(1)}, bf16[320,384]{1,0:T(8,128)(2,1)S(1)}, u32[]{:S(2)}, u32[]{:S(2)}) collective-permute-start(bf16[320,384]{1,0:T(8,128)(2,1)S(1)} %get-tuple-element.40), channel_id=1, source_target_pairs={{0,32},{32,0},{1,33},{33,1},{2,34},{34,2},{3,35},{35,3},{4,36},{36... | collective-permute-start | bytes 737288 | tf_op jit(solution)/shard_map/ppermute | solution.py:270
  58.5 3.8 %collective-permute-start.17 = (bf16[64,512]{1,0:T(8,128)(2,1)S(1)}, bf16[64,512]{1,0:T(8,128)(2,1)S(1)}, u32[]{:S(2)}, u32[]{:S(2)}) collective-permute-start(bf16[64,512]{1,0:T(8,128)(2,1)S(1)} %add_convert_fusion.3), channel_id=1, source_target_pairs={{0,24},{8,0},{16,8},{24,16},{1,25},{9,1},{17,9},{25,17},{2,26},{10... | collective-permute-start | bytes 196616 | tf_op jit(solution)/shard_map/ppermute | solution.py:270
  58.9 6.0 %collective-permute-start.16 = (bf16[64,512]{1,0:T(8,128)(2,1)S(1)}, bf16[64,512]{1,0:T(8,128)(2,1)S(1)}, u32[]{:S(2)}, u32[]{:S(2)}) collective-permute-start(bf16[64,512]{1,0:T(8,128)(2,1)S(1)} %add_convert_fusion.3), channel_id=1, source_target_pairs={{0,8},{8,16},{16,24},{24,0},{1,9},{9,17},{17,25},{25,1},{2,10},{10... | collective-permute-start | bytes 196616 | tf_op jit(solution)/shard_map/ppermute | solution.py:270
  60.1 4.8 %collective-permute-start.15 = (bf16[64,512]{1,0:T(8,128)(2,1)S(1)}, bf16[64,512]{1,0:T(8,128)(2,1)S(1)}, u32[]{:S(2)}, u32[]{:S(2)}) collective-permute-start(bf16[64,512]{1,0:T(8,128)(2,1)S(1)} %add_convert_fusion.3), channel_id=1, source_target_pairs={{0,16},{8,24},{16,0},{24,8},{1,17},{9,25},{17,1},{25,9},{2,18},{10... | collective-permute-start | bytes 196616 | tf_op jit(solution)/shard_map/ppermute | solution.py:270
  60.7 10.1 %collective-permute-start.14 = (bf16[320,384]{1,0:T(8,128)(2,1)S(1)}, bf16[320,384]{1,0:T(8,128)(2,1)S(1)}, u32[]{:S(2)}, u32[]{:S(2)}) collective-permute-start(bf16[320,384]{1,0:T(8,128)(2,1)S(1)} %add_convert_fusion.1), channel_id=1, source_target_pairs={{0,192},{64,0},{128,64},{192,128},{1,193},{65,1},{129,65},{193,129... | collective-permute-start | bytes 737288 | tf_op jit(solution)/shard_map/ppermute | solution.py:270
  62.3 10.5 %collective-permute-start.13 = (bf16[320,384]{1,0:T(8,128)(2,1)S(1)}, bf16[320,384]{1,0:T(8,128)(2,1)S(1)}, u32[]{:S(2)}, u32[]{:S(2)}) collective-permute-start(bf16[320,384]{1,0:T(8,128)(2,1)S(1)} %add_convert_fusion.1), channel_id=1, source_target_pairs={{0,64},{64,128},{128,192},{192,0},{1,65},{65,129},{129,193},{193,1... | collective-permute-start | bytes 737288 | tf_op jit(solution)/shard_map/ppermute | solution.py:270
  62.3 12.6 %collective-permute-start.12 = (bf16[320,384]{1,0:T(8,128)(2,1)S(1)}, bf16[320,384]{1,0:T(8,128)(2,1)S(1)}, u32[]{:S(2)}, u32[]{:S(2)}) collective-permute-start(bf16[320,384]{1,0:T(8,128)(2,1)S(1)} %add_convert_fusion.1), channel_id=1, source_target_pairs={{0,128},{64,192},{128,0},{192,64},{1,129},{65,193},{129,1},{193,65... | collective-permute-start | bytes 737288 | tf_op jit(solution)/shard_map/ppermute | solution.py:270
  68.0 21.4 %collective-permute-start.18 = (bf16[192,512]{1,0:T(8,128)(2,1)S(1)}, bf16[192,512]{1,0:T(8,128)(2,1)S(1)}, u32[]{:S(2)}, u32[]{:S(2)}) collective-permute-start(bf16[192,512]{1,0:T(8,128)(2,1)S(1)} %pad_maximum_fusion.g0_ref), channel_id=1, source_target_pairs={{0,64},{64,128},{128,192},{192,0},{1,65},{65,129},{129,193},{193,1... | collective-permute-start | bytes 589832 | tf_op jit(solution)/shard_map/ppermute | solution.py:270
  69.1 20.3 %collective-permute-start.19 = (bf16[192,512]{1,0:T(8,128)(2,1)S(1)}, bf16[192,512]{1,0:T(8,128)(2,1)S(1)}, u32[]{:S(2)}, u32[]{:S(2)}) collective-permute-start(bf16[192,512]{1,0:T(8,128)(2,1)S(1)} %pad_maximum_fusion.g0_ref), channel_id=1, source_target_pairs={{0,128},{64,192},{128,0},{192,64},{1,129},{65,193},{129,1},{193,65... | collective-permute-start | bytes 589832 | tf_op jit(solution)/shard_map/ppermute | solution.py:270
  70.8 18.7 %collective-permute-start.20 = (bf16[192,512]{1,0:T(8,128)(2,1)S(1)}, bf16[192,512]{1,0:T(8,128)(2,1)S(1)}, u32[]{:S(2)}, u32[]{:S(2)}) collective-permute-start(bf16[192,512]{1,0:T(8,128)(2,1)S(1)} %pad_maximum_fusion.g0_ref), channel_id=1, source_target_pairs={{0,192},{64,0},{128,64},{192,128},{1,193},{65,1},{129,65},{193,129... | collective-permute-start | bytes 589832 | tf_op jit(solution)/shard_map/ppermute | solution.py:270
  89.4 10.2 %all-to-all-start.2 = ((bf16[8,16,1024]{2,1,0:T(8,128)(2,1)}), bf16[8,16,1024]{2,1,0:T(8,128)(2,1)S(1)}, u32[]{:S(2)}, u32[]{:S(2)}) async-start(bf16[8,16,1024]{2,1,0:T(8,128)(2,1)} %shard_map.81), calls=%async_computation.2 | async-start | bytes 524288 | tf_op jit(solution)/shard_map/all_to_all | solution.py:262
